TPU v7x, 512 devices: a whole 4x4x16 slice. The times are simulated.
512 devices in a mesh: leaf: 16 (over z), row: 8 (over y, core), col: 4 (over x).
Axes of the slice: x: 4, y: 4, z: 16, core: 2. Of those that a mesh axis runs over, the one named last changes fastest.
Arguments:
- right_root: float32 [8, 4096], P(None, ('leaf', 'row')), may hold values from -6 to 6
- right_middle: float32 [8, 8192], P(None, ('leaf', 'row')), may hold values from -6 to 6
- right_lower: float32 [8, 16384], P(None, ('leaf', 'row')), may hold values from -6 to 6
- inverse_root: float32 [2, 4096, 4096], P(None, 'col', ('leaf', 'row')), may hold values from -0.09375 to 0.09375
- inverse_middle: float32 [2, 4096, 8192], P(None, 'col', ('leaf', 'row')), may hold values from -0.09375 to 0.09375
- inverse_lower: float32 [2, 4096, 16384], P(None, 'col', ('leaf', 'row')), may hold values from -0.09375 to 0.09375
- upward_middle: float32 [8192, 2048], P(('leaf', 'row'), 'col'), may hold values from -0.09375 to 0.09375
- upward_lower: float32 [16384, 2048], P(('leaf', 'row'), 'col'), may hold values from -0.09375 to 0.09375
- downward_middle: float32 [2048, 8192], P('col', ('leaf', 'row')), may hold values from -0.125 to 0.125
- downward_lower: float32 [2048, 16384], P('col', ('leaf', 'row')), may hold values from -0.125 to 0.125
- index_middle: int32 [2, 2048], P(None, 'col'), may hold values from 0 to 4095, as said below
- index_lower: int32 [4, 2048], P(None, 'col'), may hold values from 0 to 4095, as said below
Outputs:
- solution_root: float32 [8, 4096], P(None, ('leaf', 'row'))
- solution_middle: float32 [8, 8192], P(None, ('leaf', 'row'))
- solution_lower: float32 [8, 16384], P(None, ('leaf', 'row'))
Inputs may be any that keep to these rules, and one draw needn't show every extreme that they name: `index_middle`: row f lists 2048 distinct positions in the separator of the parent of middle front f; the two rows may share positions. `index_lower`: row f lists 2048 distinct positions in the separator of middle front f // 2; sibling rows may share positions.
All inputs are finite; a program needn't handle non-finite values.
Results may differ from a plain program's by a relative error of at most 0.00019.
Values sent between devices are 32-bit elements; how exact they have to be, the bound alone decides.
No kernel may reach another device: no remote copies, remote signals or barrier semaphores. Data moves between devices by JAX's collectives and lax.ppermute only.
A program may use at most 64 MiB of HBM per device.

v0:
```python
import jax
import jax.numpy as jnp
from jax import lax
from jax.sharding import PartitionSpec as P

S = 4096


def matmul_hi(left_side, right_side):
    return jnp.dot(
        left_side, right_side, precision=lax.Precision.HIGHEST, preferred_element_type=jnp.float32
    )


def local(
    right_root,
    right_middle,
    right_lower,
    inverse_root,
    inverse_middle,
    inverse_lower,
    upward_middle,
    upward_lower,
    downward_middle,
    downward_lower,
    index_middle,
    index_lower,
):
    leaves = lax.axis_size("leaf")
    col_count = lax.axis_size("col")
    leaf_at = lax.axis_index("leaf")
    col_at = lax.axis_index("col")
    quarter = S // col_count

    def col_total(partial_sum):
        return lax.psum(partial_sum, "col")

    def spread(block, fronts):
        group_size = leaves // fronts
        everything = lax.all_gather(block, ("leaf", "row"), axis=1, tiled=True)
        front_at = leaf_at // group_size
        return lax.dynamic_slice_in_dim(everything, front_at * S, S, 1)

    def collect(update, fronts):
        group_size = leaves // fronts
        front_at = leaf_at // group_size
        padded = jnp.zeros((update.shape[0], fronts * S), jnp.float32)
        padded = lax.dynamic_update_slice_in_dim(padded, update, front_at * S, 1)
        return lax.psum_scatter(padded, ("leaf", "row"), scatter_dimension=1, tiled=True)

    def solve_block(whole_front, inverses, selector):
        operand = lax.dynamic_slice_in_dim(whole_front, col_at * quarter, quarter, 1)
        return col_total(matmul_hi(operand, inverses[selector]))

    def extend_add(child_block, upward_local, index_local, fronts_parent, fronts_child):
        product = matmul_hi(child_block, upward_local)
        child_group = leaves // fronts_child
        child_at = leaf_at // child_group
        positions = index_local[child_at]
        update = jnp.zeros((child_block.shape[0], S), jnp.float32).at[:, positions].add(product)
        return col_total(collect(update, fronts_parent))

    def descend(
        parent_block,
        fronts_parent,
        child_block,
        downward_local,
        index_local,
        fronts_child,
        inverses,
    ):
        parent_front = spread(parent_block, fronts_parent)
        child_at = leaf_at // (leaves // fronts_child)
        picked = jnp.take(parent_front, index_local[child_at], axis=1)
        coupled = col_total(matmul_hi(picked, downward_local))
        reduced = child_block - coupled
        return solve_block(spread(reduced, fronts_child), inverses, 1)

    z_lower = solve_block(spread(right_lower, 4), inverse_lower, 0)
    w_middle = right_middle - extend_add(z_lower, upward_lower, index_lower, 2, 4)
    z_middle = solve_block(spread(w_middle, 2), inverse_middle, 0)
    w_root = right_root - extend_add(z_middle, upward_middle, index_middle, 1, 2)
    z_root = solve_block(spread(w_root, 1), inverse_root, 0)
    solution_root = solve_block(spread(z_root, 1), inverse_root, 1)
    solution_middle = descend(
        solution_root, 1, z_middle, downward_middle, index_middle, 2, inverse_middle
    )
    solution_lower = descend(
        solution_middle, 2, z_lower, downward_lower, index_lower, 4, inverse_lower
    )
    return (solution_root, solution_middle, solution_lower)


def solution(mesh):
    in_specs = (
        P(None, ("leaf", "row")),
        P(None, ("leaf", "row")),
        P(None, ("leaf", "row")),
        P(None, "col", ("leaf", "row")),
        P(None, "col", ("leaf", "row")),
        P(None, "col", ("leaf", "row")),
        P(("leaf", "row"), "col"),
        P(("leaf", "row"), "col"),
        P("col", ("leaf", "row")),
        P("col", ("leaf", "row")),
        P(None, "col"),
        P(None, "col"),
    )
    out_specs = (P(None, ("leaf", "row")), P(None, ("leaf", "row")), P(None, ("leaf", "row")))
    return jax.shard_map(local, mesh=mesh, in_specs=in_specs, out_specs=out_specs, check_vma=False)
```

profile of v0, /device:TPU:1, one launch (start us, length us, event | category | flops | bytes accessed | tf_op | source)
XLA Modules:
  0.0 1315.5 jit_solution(3963378891636130782)
XLA Ops:
  7.3 91.3 %all_gather.24 = f32[8,16384]{1,0:T(8,128)S(1)} all-gather(f32[8,128]{1,0:T(8,128)} %param.16), channel_id=1, replica_groups=mesh['leaf'=16,'row'=8,'col'=4] {'leaf','row'}, dimensions={1}, use_global_device_ids=true | all-gather | bytes 528384 | tf_op jit(solution)/shard_map/all_gather | solution.py:40
  100.0 8.5 psum.70
  109.6 2.8 scatter_custom_fusion
  112.9 2.6 copy.57
  117.4 246.4 %reduce-scatter.7.cloned.1.call-done = f32[64,8]{1,0:T(8,128)} async-done(((f32[8192,8]{1,0:T(8,128)}), f32[64,8]{1,0:T(8,128)}) %reduce-scatter.7.cloned.1.call-update) | async-done | bytes 2064
  364.6 8.7 psum.71
  373.3 95.1 %all-gather = f32[128,64,8]{1,2,0:T(8,128)S(1)} all-gather(f32[1,64,8]{1,2,0:T(8,128)S(1)} %subtract_bitcast_fusion.2), channel_id=1, replica_groups=mesh['leaf'=16,'row'=8,'col'=4] {'leaf','row'}, dimensions={0}, use_global_device_ids=true | all-gather | bytes 264192 | tf_op jit(solution)/shard_map/all_gather | solution.py:40
  469.0 6.0 psum.72
  475.3 3.7 scatter_custom_fusion.1
  479.6 247.5 %reduce-scatter.5.cloned.1.call-done = f32[8,32]{0,1:T(8,128)} async-done(((f32[8,4096]{0,1:T(8,128)}), f32[8,32]{0,1:T(8,128)}) %reduce-scatter.5.cloned.1.call-update) | async-done | bytes 1040 | tf_op jit(solution)/shard_map/reduce_scatter | solution.py:49
  727.1 13.7 %psum.73 = f32[8,32]{0,1:T(8,128)S(1)} all-reduce(f32[8,32]{0,1:T(8,128)} %reduce-scatter.5.cloned.1.call-done), channel_id=1, replica_groups=mesh['leaf'=16,'row'=8,'col'=4] {'col'}, use_global_device_ids=true, to_apply=%region_7.8 | all-reduce | flops 256 | bytes 2048 | tf_op jit(solution)/shard_map/psum | solution.py:36
  740.9 97.0 %all-gather.1 = f32[128,32,8]{1,2,0:T(8,128)S(1)} all-gather(f32[1,32,8]{1,2,0:T(8,128)S(1)} %copy.47), channel_id=1, replica_groups=mesh['leaf'=16,'row'=8,'col'=4] {'leaf','row'}, dimensions={0}, use_global_device_ids=true | all-gather | bytes 132096 | tf_op jit(solution)/shard_map/all_gather | solution.py:40
  838.4 6.0 psum.74
  844.5 82.8 %all-gather.2 = f32[128,32,8]{1,2,0:T(8,128)S(1)} all-gather(f32[1,32,8]{1,2,0:T(8,128)S(1)} %bitcast.89), channel_id=1, replica_groups=mesh['leaf'=16,'row'=8,'col'=4] {'leaf','row'}, dimensions={0}, use_global_device_ids=true | all-gather | bytes 132096 | tf_op jit(solution)/shard_map/all_gather | solution.py:40
  927.8 7.7 psum.75
  935.5 83.8 %all-gather.3 = f32[128,32,8]{1,2,0:T(8,128)S(1)} all-gather(f32[1,32,8]{1,2,0:T(8,128)S(1)} %bitcast.87), channel_id=1, replica_groups=mesh['leaf'=16,'row'=8,'col'=4] {'leaf','row'}, dimensions={0}, use_global_device_ids=true | all-gather | bytes 132096 | tf_op jit(solution)/shard_map/all_gather | solution.py:40
  1022.4 6.0 psum.76
  1028.4 82.8 %all-gather.4 = f32[128,64,8]{1,2,0:T(8,128)S(1)} all-gather(f32[1,64,8]{1,2,0:T(8,128)S(1)} %subtract_bitcast_fusion.1), channel_id=1, replica_groups=mesh['leaf'=16,'row'=8,'col'=4] {'leaf','row'}, dimensions={0}, use_global_device_ids=true | all-gather | bytes 264192 | tf_op jit(solution)/shard_map/all_gather | solution.py:40
  1111.8 7.8 psum.77
  1119.6 83.6 %all-gather.5 = f32[128,64,8]{1,2,0:T(8,128)S(1)} all-gather(f32[1,64,8]{1,2,0:T(8,128)S(1)} %bitcast.88), channel_id=1, replica_groups=mesh['leaf'=16,'row'=8,'col'=4] {'leaf','row'}, dimensions={0}, use_global_device_ids=true | all-gather | bytes 264192 | tf_op jit(solution)/shard_map/all_gather | solution.py:40
  1203.2 2.6 copy.56
  1210.9 6.0 psum.78
  1216.9 83.0 %all_gather.31 = f32[8,16384]{1,0:T(8,128)S(1)} all-gather(f32[8,128]{1,0:T(8,128)S(1)} %sub.36), channel_id=1, replica_groups=mesh['leaf'=16,'row'=8,'col'=4] {'leaf','row'}, dimensions={1}, use_global_device_ids=true | all-gather | bytes 528384 | tf_op jit(solution)/shard_map/all_gather | solution.py:40
  1300.3 8.3 psum.79
  (67 shorter events, 17.6 us)
Async XLA Ops:
  7.2 101.3 %copy-start = (f32[128,512]{1,0:T(8,128)S(1)}, f32[128,512]{1,0:T(8,128)}, u32[]{:S(2)}) copy-start(f32[128,512]{1,0:T(8,128)} %param.21) | copy-start | bytes 786436
  7.2 356.6 %reduce-scatter.7.cloned.1.call-start = ((), (), s32[]{:S(2)}) async-start(), calls=%async_computation.3 | async-start | bytes 4227072
  115.5 0.7 copy-start.8
  115.5 257.7 %copy-start.9 = (f32[8,64]{1,0:T(8,128)S(1)}, f32[8,64]{1,0:T(8,128)}, u32[]{:S(2)}) copy-start(f32[8,64]{1,0:T(8,128)} %param.15) | copy-start | bytes 6148
  115.6 353.1 %copy-start.2 = (f32[2,1024,64]{1,2,0:T(8,128)S(1)}, f32[2,1024,64]{1,2,0:T(8,128)}, u32[]{:S(2)}) copy-start(f32[2,1024,64]{1,2,0:T(8,128)} %param.18) | copy-start | bytes 1572868
  115.6 359.5 %copy-start.4 = (f32[64,512]{1,0:T(8,128)S(1)}, f32[64,512]{1,0:T(8,128)}, u32[]{:S(2)}) copy-start(f32[64,512]{1,0:T(8,128)} %param.20) | copy-start | bytes 393220
  115.6 611.5 %reduce-scatter.5.cloned.1.call-start = ((), (), s32[]{:S(2)}) async-start(), calls=%async_computation.2 | async-start | bytes 2113536 | tf_op jit(solution)/shard_map/reduce_scatter | solution.py:49
  479.0 359.2 %copy-start.3 = (f32[2,1024,32]{1,2,0:T(8,128)S(1)}, f32[2,1024,32]{1,2,0:T(8,128)}, u32[]{:S(2)}) copy-start(f32[2,1024,32]{1,2,0:T(8,128)} %param.17) | copy-start | bytes 786436
  927.3 93.8 %copy-start.5 = (f32[512,64]{0,1:T(8,128)S(1)}, f32[512,64]{0,1:T(8,128)}, u32[]{:S(2)}) copy-start(f32[512,64]{0,1:T(8,128)} %param.22) | copy-start | bytes 393220
  935.5 175.7 %copy-start.6 = (f32[8,32]{1,0:T(8,128)}, f32[8,32]{1,0:T(8,128)S(1)}, u32[]{:S(2)}) copy-start(f32[8,32]{1,0:T(8,128)S(1)} %psum.75) | copy-start | bytes 3076
  1119.6 86.2 %copy-start.7 = (f32[8,64]{1,0:T(8,128)}, f32[8,64]{1,0:T(8,128)S(1)}, u32[]{:S(2)}) copy-start(f32[8,64]{1,0:T(8,128)S(1)} %psum.77) | copy-start | bytes 6148
  1205.8 3.5 copy-start.10
  1205.8 94.2 %copy-start.1 = (f32[2,1024,128]{2,1,0:T(8,128)S(1)}, f32[2,1024,128]{2,1,0:T(8,128)}, u32[]{:S(2)}) copy-start(f32[2,1024,128]{2,1,0:T(8,128)} %param.19) | copy-start | bytes 3145732
Sparse Core Ops, SparseCore 0:
  115.7 248.0 reduce-scatter.6
  479.2 247.8 reduce-scatter.4
where the time goes:
time: 1320 us
  blocking collectives  778 us (59%)
  waiting for transfers between devices  494 us (37%)
  between operations  14.3 us (1%)
  local copies, waits for them, and re-layouts  14.1 us (1%)
    all_gather x8, blocking collectives, spread(): everything = lax.all_gather(block, ('leaf', 'row'), axis=1, tiled=True)  699 us
    reduce_scatter x1, waiting for transfers between devices, collect(): lax.psum_scatter(padded, ('leaf', 'row'), scatter_dimension=1, tiled=True)  248 us
    unnamed x3, waiting for transfers between devices  246 us
    psum x10, blocking collectives, col_total(): return lax.psum(partial_sum, 'col')  78.7 us
  transfers between devices with their start and end apart: 2, of which 2 were waited for; matrix products, arithmetic and copies ran while one was open for 0% of the time, Pallas kernels for 0%

commit v1 on v0

v1 whole, which is shorter than its diff:
```python
import jax
import jax.numpy as jnp
from jax import lax
from jax.sharding import Mesh
from jax.sharding import PartitionSpec as P

S = 4096
QUARTER = 1024
SIZES = {"a": 2, "b": 2, "d": 4, "y": 4, "k": 2, "x": 4}


def count(axes):
    total = 1
    for axis in axes:
        total *= SIZES[axis]
    return total


def matmul_hi(left_side, right_side):
    return jnp.dot(
        left_side, right_side, precision=lax.Precision.HIGHEST, preferred_element_type=jnp.float32
    )


def exchange(pieces, axes):
    return lax.all_to_all(pieces, tuple(axes), 0, 0, tiled=False)


def gather(block, axes):
    return exchange(jnp.broadcast_to(block[None], (count(axes),) + block.shape), axes)


def total(block, axes):
    return jnp.sum(gather(block, axes), axis=0)


def flat(pieces):
    return pieces.transpose(1, 0, 2).reshape(pieces.shape[1], -1)


def quarter_of(pieces):
    x_at = lax.axis_index("x")
    parts = pieces.reshape((4, pieces.shape[0] // 4) + pieces.shape[1:])
    return flat(lax.dynamic_index_in_dim(parts, x_at, 0, keepdims=False))


def extend(product, positions, right_block, at, level_axes):
    first = (lax.axis_index("x") == 0).astype(jnp.float32)
    update = jnp.zeros((8, S), jnp.float32)
    update = lax.dynamic_update_slice_in_dim(update, right_block * first, at * right_block.shape[1], 1)
    update = update.at[:, positions].add(-product)
    pieces = update.reshape(8, 4, 8, 128).transpose(2, 1, 0, 3).reshape(32, 8, 128)
    own = jnp.sum(exchange(pieces, "ykx"), axis=0)
    own = total(own, level_axes)
    return flat(gather(own, "yk"))


def local(
    right_root,
    right_middle,
    right_lower,
    inverse_root,
    inverse_middle,
    inverse_lower,
    upward_middle,
    upward_lower,
    downward_middle,
    downward_lower,
    index_middle,
    index_lower,
):
    at = lax.axis_index
    front_middle = at("a")
    front_lower = at(("a", "b"))
    positions_middle = lax.dynamic_index_in_dim(index_middle, front_middle, 0, keepdims=False)
    positions_lower = lax.dynamic_index_in_dim(index_lower, front_lower, 0, keepdims=False)

    operand = quarter_of(gather(right_lower, "dyk"))
    z_lower = total(matmul_hi(operand, inverse_lower[0]), "x")
    w_middle = extend(
        matmul_hi(z_lower, upward_lower), positions_lower, right_middle, at(("b", "d", "y", "k")), "bd"
    )
    z_middle = total(matmul_hi(w_middle, inverse_middle[0]), "x")
    w_root = extend(
        matmul_hi(z_middle, upward_middle),
        positions_middle,
        right_root,
        at(("a", "b", "d", "y", "k")),
        "abd",
    )
    z_root = total(matmul_hi(w_root, inverse_root[0]), "x")
    operand = quarter_of(gather(z_root, "abdyk"))
    solution_root = total(matmul_hi(operand, inverse_root[1]), "x")
    whole = flat(gather(solution_root, "abdyk"))
    picked = jnp.take(whole, positions_middle, axis=1)
    v_middle = z_middle - total(matmul_hi(picked, downward_middle), "x")
    operand = quarter_of(gather(v_middle, "bdyk"))
    solution_middle = total(matmul_hi(operand, inverse_middle[1]), "x")
    whole = flat(gather(solution_middle, "bdyk"))
    picked = jnp.take(whole, positions_lower, axis=1)
    v_lower = z_lower - total(matmul_hi(picked, downward_lower), "x")
    operand = quarter_of(gather(v_lower, "dyk"))
    solution_lower = total(matmul_hi(operand, inverse_lower[1]), "x")
    return (solution_root, solution_middle, solution_lower)


def solution(mesh):
    split = Mesh(mesh.devices.reshape(tuple(SIZES.values())), tuple(SIZES))
    n = ("a", "b", "d", "y", "k")
    in_specs = (
        P(None, n),
        P(None, n),
        P(None, n),
        P(None, "x", n),
        P(None, "x", n),
        P(None, "x", n),
        P(n, "x"),
        P(n, "x"),
        P("x", n),
        P("x", n),
        P(None, "x"),
        P(None, "x"),
    )
    out_specs = (P(None, n), P(None, n), P(None, n))
    return jax.shard_map(local, mesh=split, in_specs=in_specs, out_specs=out_specs, check_vma=False)
```

time: 1320 us -> 295 us (0.22)
  blocking collectives: 778 us -> 168 us
  waiting for transfers between devices: 494 us -> 48.1 us
  starting transfers between devices: 0.08 us -> 37.3 us
  between operations: 14.3 us -> 1.05 us
    all_gather x8 -> x0, blocking collectives: 699 us -> none  [spread(): everything = lax.all_gather(block, ('leaf', 'row'), axis=1, tiled=True)]
    reduce_scatter x1 -> x0, waiting for transfers between devices: 248 us -> none  [collect(): lax.psum_scatter(padded, ('leaf', 'row'), scatter_dimension=1, tiled=True)]
    unnamed x3 -> x0, waiting for transfers between devices: 246 us -> none
    all_to_all x0 -> x14, blocking collectives: none -> 168 us  [exchange(): return lax.all_to_all(pieces, tuple(axes), 0, 0, tiled=False)]
    psum x10 -> x0, blocking collectives: 78.7 us -> none  [col_total(): return lax.psum(partial_sum, 'col')]
    all_to_all x0 -> x6, waiting for transfers between devices: none -> 48.1 us  [exchange(): return lax.all_to_all(pieces, tuple(axes), 0, 0, tiled=False)]
    all_to_all x0 -> x6, starting transfers between devices: none -> 37.3 us  [exchange(): return lax.all_to_all(pieces, tuple(axes), 0, 0, tiled=False)]
  transfers between devices with their start and end apart: 2 -> 6, of which waited for: 2 -> 6; matrix products, arithmetic and copies ran while one was open for 0% -> 1% of each run, Pallas kernels for 0% -> 0%
where the time goes in v1:
time: 295 us; the launch traced here: 294 us
  blocking collectives  168 us (57%)
  waiting for transfers between devices  48.1 us (16%)
  starting transfers between devices  37.3 us (13%)
  other arithmetic  17.8 us (6%)
  local copies, waits for them, and re-layouts  16.5 us (6%)
  matrix products  4.97 us (2%)
    all_to_all x14, blocking collectives, exchange(): return lax.all_to_all(pieces, tuple(axes), 0, 0, tiled=False)  168 us
    all_to_all x6, waiting for transfers between devices, exchange(): return lax.all_to_all(pieces, tuple(axes), 0, 0, tiled=False)  48.1 us
    all_to_all x6, starting transfers between devices, exchange(): return lax.all_to_all(pieces, tuple(axes), 0, 0, tiled=False)  37.3 us
    scatter-add x2, other arithmetic, extend(): update = update.at[:, positions].add(-product)  8.12 us
    all_to_all x9, other arithmetic, exchange(): return lax.all_to_all(pieces, tuple(axes), 0, 0, tiled=False)  6.38 us
  transfers between devices with their start and end apart: 6, of which 6 were waited for; matrix products, arithmetic and copies ran while one was open for 1% of the time, Pallas kernels for 0%

profile of v1, /device:TPU:1, one launch (start us, length us, event | category | flops | bytes accessed | tf_op | source)
XLA Modules:
  0.0 294.1 jit_solution(12578391820258354575)
XLA Ops:
  2.1 10.4 %all-to-all-start = ((f32[32,8,128]{2,1,0:T(8,128)}), f32[32,8,128]{2,1,0:T(8,128)S(1)}, u32[]{:S(2)}, u32[]{:S(2)}) async-start(f32[32,8,128]{2,1,0:T(8,128)} %broadcast_in_dim.42), calls=%async_computation | async-start | bytes 262144 | tf_op jit(solution)/shard_map/all_to_all | solution.py:26
  14.6 6.5 %all-to-all-done = f32[32,8,128]{2,1,0:T(8,128)S(1)} async-done(((f32[32,8,128]{2,1,0:T(8,128)}), f32[32,8,128]{2,1,0:T(8,128)S(1)}, u32[]{:S(2)}, u32[]{:S(2)}) %all-to-all-start) | async-done | bytes 131104 | tf_op jit(solution)/shard_map/all_to_all | solution.py:26
  30.4 4.1 %scatter_fusion = f32[8,4096]{0,1:T(8,128)S(1)} fusion(f32[8,4096]{0,1:T(8,128)S(1)} %constant_dynamic-update-slice_fusion, s32[512]{0:T(512)S(1)} %bitcast.111, f32[512,8]{1,0:T(8,128)S(1)} %copy.80), kind=kCustom, calls=%fused_computation.2 | custom fusion | flops 4096 | bytes 51200 | tf_op jit(solution)/shard_map/scatter-add | solution.py:51
  35.1 12.5 %all_to_all.104 = f32[32,8,128]{2,1,0:T(8,128)S(1)} all-to-all(f32[32,8,128]{2,1,0:T(8,128)S(1)} %bitcast.100), channel_id=1, replica_groups=mesh['a'=2,'b'=2,'d'=4,'y'=4,'k'=2,'x'=4] {'y','k','x'}, dimensions={0} | all-to-all | bytes 262144 | tf_op jit(solution)/shard_map/all_to_all | solution.py:26
  47.6 18.4 %all_to_all.105 = f32[8,8,128]{2,1,0:T(8,128)S(1)} all-to-all(f32[8,8,128]{2,1,0:T(8,128)S(1)} %broadcast_in_dim.44), channel_id=1, replica_groups=mesh['a'=2,'b'=2,'d'=4,'y'=4,'k'=2,'x'=4] {'b','d'}, dimensions={0} | all-to-all | bytes 65536 | tf_op jit(solution)/shard_map/all_to_all | solution.py:26
  66.6 4.9 %all-to-all-start.4 = ((f32[8,8,128]{2,1,0:T(8,128)}), f32[8,8,128]{2,1,0:T(8,128)S(1)}, u32[]{:S(2)}, u32[]{:S(2)}) async-start(f32[8,8,128]{2,1,0:T(8,128)} %broadcast_in_dim.45), calls=%async_computation.4 | async-start | bytes 65536 | tf_op jit(solution)/shard_map/all_to_all | solution.py:26
  71.6 4.6 %all-to-all-done.4 = f32[8,8,128]{2,1,0:T(8,128)S(1)} async-done(((f32[8,8,128]{2,1,0:T(8,128)}), f32[8,8,128]{2,1,0:T(8,128)S(1)}, u32[]{:S(2)}, u32[]{:S(2)}) %all-to-all-start.4) | async-done | bytes 32800 | tf_op jit(solution)/shard_map/all_to_all | solution.py:26
  86.2 4.1 %scatter_fusion.1 = f32[8,4096]{0,1:T(8,128)S(1)} fusion(f32[8,4096]{0,1:T(8,128)S(1)} %constant_dynamic-update-slice_fusion.1, s32[512]{0:T(512)S(1)} %bitcast.110, f32[512,8]{1,0:T(8,128)S(1)} %copy.82), kind=kCustom, calls=%fused_computation.3 | custom fusion | flops 4096 | bytes 51200 | tf_op jit(solution)/shard_map/scatter-add | solution.py:51
  90.8 12.5 %all_to_all.106 = f32[32,8,128]{2,1,0:T(8,128)S(1)} all-to-all(f32[32,8,128]{2,1,0:T(8,128)S(1)} %bitcast.101), channel_id=1, replica_groups=mesh['a'=2,'b'=2,'d'=4,'y'=4,'k'=2,'x'=4] {'y','k','x'}, dimensions={0} | all-to-all | bytes 262144 | tf_op jit(solution)/shard_map/all_to_all | solution.py:26
  103.3 18.8 %all_to_all.107 = f32[16,8,128]{2,1,0:T(8,128)S(1)} all-to-all(f32[16,8,128]{2,1,0:T(8,128)S(1)} %broadcast_in_dim.47), channel_id=1, replica_groups=mesh['a'=2,'b'=2,'d'=4,'y'=4,'k'=2,'x'=4] {'a','b','d'}, dimensions={0} | all-to-all | bytes 131072 | tf_op jit(solution)/shard_map/all_to_all | solution.py:26
  122.2 9.2 %all_to_all.100 = f32[8,8,128]{2,1,0:T(8,128)S(1)} all-to-all(f32[8,8,128]{2,1,0:T(8,128)S(1)} %broadcast_in_dim.48), channel_id=1, replica_groups=mesh['a'=2,'b'=2,'d'=4,'y'=4,'k'=2,'x'=4] {'y','k'}, dimensions={0} | all-to-all | bytes 65536 | tf_op jit(solution)/shard_map/all_to_all | solution.py:26
  131.7 6.5 %all_to_all.108 = f32[4,1,256]{2,1,0:T(1,128)S(1)} all-to-all(f32[4,1,256]{2,1,0:T(1,128)S(1)} %reshape.197), channel_id=1, replica_groups=mesh['a'=2,'b'=2,'d'=4,'y'=4,'k'=2,'x'=4] {'x'}, dimensions={0} | all-to-all | bytes 8192 | tf_op jit(solution)/shard_map/all_to_all | solution.py:26
  139.1 22.9 %all_to_all.101 = f32[128,1,256]{2,1,0:T(1,128)S(1)} all-to-all(f32[128,1,256]{2,1,0:T(1,128)S(1)} %reshape.199), channel_id=1, replica_groups=mesh['a'=2,'b'=2,'d'=4,'y'=4,'k'=2,'x'=4] {'a','b','d','y','k'}, dimensions={0} | all-to-all | bytes 262144 | tf_op jit(solution)/shard_map/all_to_all | solution.py:26
  163.6 6.5 %all_to_all.109 = f32[4,1,256]{2,1,0:T(1,128)S(1)} all-to-all(f32[4,1,256]{2,1,0:T(1,128)S(1)} %reshape.201), channel_id=1, replica_groups=mesh['a'=2,'b'=2,'d'=4,'y'=4,'k'=2,'x'=4] {'x'}, dimensions={0} | all-to-all | bytes 8192 | tf_op jit(solution)/shard_map/all_to_all | solution.py:26
  171.7 8.1 %all-to-all-start.12 = ((f32[128,1,256]{2,1,0:T(1,128)}), f32[128,1,256]{2,1,0:T(1,128)S(1)}, u32[]{:S(2)}, u32[]{:S(2)}) async-start(f32[128,1,256]{2,1,0:T(1,128)} %reshape.203), calls=%async_computation.12 | async-start | bytes 262144 | tf_op jit(solution)/shard_map/all_to_all | solution.py:26
  180.9 14.9 %all-to-all-done.12 = f32[128,1,256]{2,1,0:T(1,128)S(1)} async-done(((f32[128,1,256]{2,1,0:T(1,128)}), f32[128,1,256]{2,1,0:T(1,128)S(1)}, u32[]{:S(2)}, u32[]{:S(2)}) %all-to-all-start.12) | async-done | bytes 131104 | tf_op jit(solution)/shard_map/all_to_all | solution.py:26
  200.0 6.5 %all_to_all.110 = f32[4,1,512]{2,1,0:T(1,128)S(1)} all-to-all(f32[4,1,512]{2,1,0:T(1,128)S(1)} %reshape.205), channel_id=1, replica_groups=mesh['a'=2,'b'=2,'d'=4,'y'=4,'k'=2,'x'=4] {'x'}, dimensions={0} | all-to-all | bytes 16384 | tf_op jit(solution)/shard_map/all_to_all | solution.py:26
  207.4 22.0 %all_to_all.102 = f32[64,1,512]{2,1,0:T(1,128)S(1)} all-to-all(f32[64,1,512]{2,1,0:T(1,128)S(1)} %reshape.207), channel_id=1, replica_groups=mesh['a'=2,'b'=2,'d'=4,'y'=4,'k'=2,'x'=4] {'b','d','y','k'}, dimensions={0} | all-to-all | bytes 262144 | tf_op jit(solution)/shard_map/all_to_all | solution.py:26
  230.8 6.5 %all_to_all.111 = f32[4,1,512]{2,1,0:T(1,128)S(1)} all-to-all(f32[4,1,512]{2,1,0:T(1,128)S(1)} %reshape.209), channel_id=1, replica_groups=mesh['a'=2,'b'=2,'d'=4,'y'=4,'k'=2,'x'=4] {'x'}, dimensions={0} | all-to-all | bytes 16384 | tf_op jit(solution)/shard_map/all_to_all | solution.py:26
  238.9 6.9 %all-to-all-start.16 = ((f32[64,1,512]{2,1,0:T(1,128)}), f32[64,1,512]{2,1,0:T(1,128)S(1)}, u32[]{:S(2)}, u32[]{:S(2)}) async-start(f32[64,1,512]{2,1,0:T(1,128)} %reshape.211), calls=%async_computation.16 | async-start | bytes 262144 | tf_op jit(solution)/shard_map/all_to_all | solution.py:26
  245.8 14.6 %all-to-all-done.16 = f32[64,1,512]{2,1,0:T(1,128)S(1)} async-done(((f32[64,1,512]{2,1,0:T(1,128)}), f32[64,1,512]{2,1,0:T(1,128)S(1)}, u32[]{:S(2)}, u32[]{:S(2)}) %all-to-all-start.16) | async-done | bytes 131104 | tf_op jit(solution)/shard_map/all_to_all | solution.py:26
  267.0 6.6 %all_to_all.112 = f32[4,8,128]{2,1,0:T(8,128)S(1)} all-to-all(f32[4,8,128]{2,1,0:T(8,128)S(1)} %broadcast_in_dim.60), channel_id=1, replica_groups=mesh['a'=2,'b'=2,'d'=4,'y'=4,'k'=2,'x'=4] {'x'}, dimensions={0} | all-to-all | bytes 32768 | tf_op jit(solution)/shard_map/all_to_all | solution.py:26
  273.6 12.9 %all_to_all.103 = f32[32,8,128]{2,1,0:T(8,128)S(1)} all-to-all(f32[32,8,128]{2,1,0:T(8,128)S(1)} %broadcast_in_dim.61), channel_id=1, replica_groups=mesh['a'=2,'b'=2,'d'=4,'y'=4,'k'=2,'x'=4] {'d','y','k'}, dimensions={0} | all-to-all | bytes 262144 | tf_op jit(solution)/shard_map/all_to_all | solution.py:26
  286.9 6.6 %all_to_all.113 = f32[4,8,128]{2,1,0:T(8,128)S(1)} all-to-all(f32[4,8,128]{2,1,0:T(8,128)S(1)} %broadcast_in_dim.62), channel_id=1, replica_groups=mesh['a'=2,'b'=2,'d'=4,'y'=4,'k'=2,'x'=4] {'x'}, dimensions={0} | all-to-all | bytes 32768 | tf_op jit(solution)/shard_map/all_to_all | solution.py:26
  (131 shorter events, 45.6 us)
Async XLA Ops:
  0.6 29.4 %copy-start = (f32[128,512]{1,0:T(8,128)S(1)}, f32[128,512]{1,0:T(8,128)}, u32[]{:S(2)}) copy-start(f32[128,512]{1,0:T(8,128)} %param.21) | copy-start | bytes 786436
  0.6 20.5 %copy-start.1 = (f32[2,1024,128]{2,1,0:T(8,128)S(1)}, f32[2,1024,128]{2,1,0:T(8,128)}, u32[]{:S(2)}) copy-start(f32[2,1024,128]{2,1,0:T(8,128)} %param.19) | copy-start | bytes 3145732
  0.7 25.2 %copy-start.13 = (s32[2,512]{1,0:T(2,128)S(1)}, s32[2,512]{1,0:T(2,128)}, u32[]{:S(2)}) copy-start(s32[2,512]{1,0:T(2,128)} %param.24) | copy-start | bytes 12292
  2.1 19.1 %all-to-all-start = ((f32[32,8,128]{2,1,0:T(8,128)}), f32[32,8,128]{2,1,0:T(8,128)S(1)}, u32[]{:S(2)}, u32[]{:S(2)}) async-start(f32[32,8,128]{2,1,0:T(8,128)} %broadcast_in_dim.42), calls=%async_computation | async-start | bytes 262144 | tf_op jit(solution)/shard_map/all_to_all | solution.py:26
  13.9 0.8 copy-start.8
  21.5 50.0 %copy-start.12 = (f32[8,32]{1,0:T(8,128)S(1)}, f32[8,32]{1,0:T(8,128)}, u32[]{:S(2)}) copy-start(f32[8,32]{1,0:T(8,128)} %param.14) | copy-start | bytes 3076
  21.5 54.8 %copy-start.3 = (f32[2,1024,64]{1,2,0:T(8,128)S(1)}, f32[2,1024,64]{1,2,0:T(8,128)}, u32[]{:S(2)}) copy-start(f32[2,1024,64]{1,2,0:T(8,128)} %param.18) | copy-start | bytes 1572868
  22.1 7.9 %all-to-all-start.1 = ((f32[4,8,128]{2,1,0:T(8,128)}), f32[4,8,128]{2,1,0:T(8,128)S(1)}, u32[]{:S(2)}, u32[]{:S(2)}) async-start(f32[4,8,128]{2,1,0:T(8,128)} %broadcast_in_dim.43), calls=%async_computation.1 | async-start | bytes 32768 | tf_op jit(solution)/shard_map/all_to_all | solution.py:26
  35.1 50.8 %copy-start.6 = (f32[64,512]{1,0:T(8,128)S(1)}, f32[64,512]{1,0:T(8,128)}, u32[]{:S(2)}) copy-start(f32[64,512]{1,0:T(8,128)} %param.20) | copy-start | bytes 393220
  66.6 9.7 %all-to-all-start.4 = ((f32[8,8,128]{2,1,0:T(8,128)}), f32[8,8,128]{2,1,0:T(8,128)S(1)}, u32[]{:S(2)}, u32[]{:S(2)}) async-start(f32[8,8,128]{2,1,0:T(8,128)} %broadcast_in_dim.45), calls=%async_computation.4 | async-start | bytes 65536 | tf_op jit(solution)/shard_map/all_to_all | solution.py:26
  77.3 7.4 %all-to-all-start.5 = ((f32[4,1,512]{2,1,0:T(1,128)}), f32[4,1,512]{2,1,0:T(1,128)S(1)}, u32[]{:S(2)}, u32[]{:S(2)}) async-start(f32[4,1,512]{2,1,0:T(1,128)} %reshape.195), calls=%async_computation.5 | async-start | bytes 16384 | tf_op jit(solution)/shard_map/all_to_all | solution.py:26
  80.7 50.7 %copy-start.5 = (f32[2,1024,32]{1,2,0:T(8,128)S(1)}, f32[2,1024,32]{1,2,0:T(8,128)}, u32[]{:S(2)}) copy-start(f32[2,1024,32]{1,2,0:T(8,128)} %param.17) | copy-start | bytes 786436
  170.7 26.2 %copy-start.9 = (f32[8,32]{1,0:T(8,128)}, f32[8,32]{1,0:T(8,128)S(1)}, u32[]{:S(2)}) copy-start(f32[8,32]{1,0:T(8,128)S(1)} %reduce_sum.115) | copy-start | bytes 3076
  171.7 26.9 %copy-start.7 = (f32[512,64]{0,1:T(8,128)S(1)}, f32[512,64]{0,1:T(8,128)}, u32[]{:S(2)}) copy-start(f32[512,64]{0,1:T(8,128)} %param.22) | copy-start | bytes 393220
  171.7 24.2 %all-to-all-start.12 = ((f32[128,1,256]{2,1,0:T(1,128)}), f32[128,1,256]{2,1,0:T(1,128)S(1)}, u32[]{:S(2)}, u32[]{:S(2)}) async-start(f32[128,1,256]{2,1,0:T(1,128)} %reshape.203), calls=%async_computation.12 | async-start | bytes 262144 | tf_op jit(solution)/shard_map/all_to_all | solution.py:26
  180.9 16.6 %copy-start.11 = (s32[1024]{0:T(1024)S(1)}, s32[1024]{0:T(1024)}, u32[]{:S(2)}) copy-start(s32[1024]{0:T(1024)} %pad_clamp_fusion.1) | copy-start | bytes 12292
  196.9 33.6 %copy-start.4 = (f32[2,1024,64]{1,2,0:T(8,128)S(1)}, f32[2,1024,64]{1,2,0:T(8,128)}, u32[]{:S(2)}) copy-start(f32[2,1024,64]{1,2,0:T(8,128)} %param.18) | copy-start | bytes 1572868
  238.0 29.0 %copy-start.10 = (f32[8,64]{1,0:T(8,128)}, f32[8,64]{1,0:T(8,128)S(1)}, u32[]{:S(2)}) copy-start(f32[8,64]{1,0:T(8,128)S(1)} %reduce_sum.117) | copy-start | bytes 6148
  238.9 21.5 %all-to-all-start.16 = ((f32[64,1,512]{2,1,0:T(1,128)}), f32[64,1,512]{2,1,0:T(1,128)S(1)}, u32[]{:S(2)}, u32[]{:S(2)}) async-start(f32[64,1,512]{2,1,0:T(1,128)} %reshape.211), calls=%async_computation.16 | async-start | bytes 262144 | tf_op jit(solution)/shard_map/all_to_all | solution.py:26
  245.8 40.7 %copy-start.2 = (f32[2,1024,128]{2,1,0:T(8,128)S(1)}, f32[2,1024,128]{2,1,0:T(8,128)}, u32[]{:S(2)}) copy-start(f32[2,1024,128]{2,1,0:T(8,128)} %param.19) | copy-start | bytes 3145732

commit v2 on v1

v2 whole, which is shorter than its diff:
```python
import functools

import jax
import jax.numpy as jnp
from jax import lax
from jax.experimental import pallas as pl
from jax.experimental.pallas import tpu as pltpu
from jax.sharding import Mesh
from jax.sharding import PartitionSpec as P

S = 4096
QUARTER = 1024
LANES = 128
SIZES = {"a": 2, "b": 2, "d": 4, "y": 4, "k": 2, "x": 4}
VMEM_LIMIT = 32 * 1024 * 1024


def count(axes):
    total = 1
    for axis in axes:
        total *= SIZES[axis]
    return total


def exchange(pieces, axes):
    return lax.all_to_all(pieces, tuple(axes), 0, 0, tiled=False)


def call(body, out_shapes, *operands, after=()):
    shapes = [jax.ShapeDtypeStruct(shape, jnp.float32) for shape in out_shapes]
    whole = pl.BlockSpec(memory_space=pltpu.VMEM)
    extra = len(after)
    return pl.pallas_call(
        lambda *refs: body(*refs[extra:]),
        out_shape=shapes[0] if len(shapes) == 1 else tuple(shapes),
        in_specs=[pl.BlockSpec(memory_space=pl.ANY)] * extra + [whole] * len(operands),
        out_specs=whole if len(shapes) == 1 else (whole,) * len(shapes),
        compiler_params=pltpu.CompilerParams(vmem_limit_bytes=VMEM_LIMIT),
    )(*after, *operands)


def product(left_side, right_side, transposed=False):
    def part(one, two):
        dims = (((1,), (1 if transposed else 0,)), ((), ()))
        return lax.dot_general(one, two, dims, preferred_element_type=jnp.float32)

    rows = left_side.shape[0]
    left_high = left_side.astype(jnp.bfloat16)
    left_low = (left_side - left_high.astype(jnp.float32)).astype(jnp.bfloat16)
    right_high = right_side.astype(jnp.bfloat16)
    right_low = (right_side - right_high.astype(jnp.float32)).astype(jnp.bfloat16)
    both = part(jnp.concatenate([left_high, left_low], axis=0), right_high)
    return both[:rows] + both[rows:] + part(left_high, right_low)


def spread(out_ref, value):
    for piece in range(out_ref.shape[0]):
        out_ref[piece] = value


def lane_ids():
    return lax.broadcasted_iota(jnp.int32, (8, LANES), 1)


def select_lanes(tiles, tile_at, lane_at):
    total = jnp.zeros((8, LANES), jnp.float32)
    for number, tile in enumerate(tiles):
        moved = jnp.take_along_axis(tile, lane_at, axis=1, mode="promise_in_bounds")
        total = jnp.where(tile_at == number, moved, total)
    return total


def row_of(index_ref, row):
    return jnp.broadcast_to(index_ref[row : row + 1, :], (8, LANES))


def sum_spread(parts_ref, out_ref):
    spread(out_ref, jnp.sum(parts_ref[...], axis=0))


def sum_only(parts_ref, out_ref):
    out_ref[...] = jnp.sum(parts_ref[...], axis=0)


def subtract_spread(parts_ref, kept_ref, out_ref):
    spread(out_ref, kept_ref[...] - jnp.sum(parts_ref[...], axis=0))


def sum_over_x(parts_ref):
    return [
        parts_ref[4 * i] + parts_ref[4 * i + 1] + parts_ref[4 * i + 2] + parts_ref[4 * i + 3]
        for i in range(8)
    ]


def regroup(sources):
    group = lane_ids() // 32
    total = jnp.zeros((8, LANES), jnp.float32)
    for to, (tile, start) in enumerate(sources):
        shift = ((to - start) * 32) % LANES
        moved = pltpu.roll(tile, shift, 1) if shift else tile
        total = jnp.where(group == to, moved, total)
    return total


def start(right_ref, root_ref, coupling_ref, out_ref, planes_ref):
    spread(out_ref, right_ref[...])
    planes_ref[:32] = root_ref[0]
    planes_ref[32:64] = root_ref[1]
    planes_ref[64:, :512] = coupling_ref[:32]
    planes_ref[64:, 512:] = coupling_ref[32:]


def lower_product(parts_ref, weights_ref, out_ref):
    x_at = lax.axis_index("x")
    operand = jnp.concatenate([parts_ref[x_at * 8 + i] for i in range(8)], axis=1)
    spread(out_ref, product(operand, weights_ref[...]))


def lower_product_copy(parts_ref, weights_ref, middle_ref, out_ref, copy_ref):
    lower_product(parts_ref, weights_ref, out_ref)
    copy_ref[...] = middle_ref[1]


def middle_product(parts_ref, weights_ref, out_ref):
    operand = jnp.concatenate([parts_ref[i] for i in range(8)], axis=1)
    doubled = jnp.concatenate([weights_ref[...], weights_ref[...]], axis=0)
    spread(out_ref, product(operand, doubled, True))


def extend(width, per_tile, parts_ref, weights_ref, source_ref, right_ref, out_ref, kept_ref):
    value = jnp.sum(parts_ref[...], axis=0)
    kept_ref[...] = value
    update = product(value[:, :width], weights_ref[...])
    tiles = [update[:, i * LANES : (i + 1) * LANES] for i in range(4)]
    for tile in range(32):
        source = row_of(source_ref, tile)
        out_ref[(tile % 8) * 4 + tile // 8] = -select_lanes(tiles, source >> 7, source & 127)
    if per_tile == 2:
        block_at = lax.axis_index(("b", "d", "y", "k"))
    else:
        block_at = lax.axis_index(("a", "b", "d", "y", "k"))
    tile_at = block_at // per_tile
    piece_at = (tile_at % 8) * 4 + tile_at // 8
    out_ref[piece_at] = out_ref[piece_at] + right_ref[...]


def stack_spread(parts_ref, kept_ref, out_ref):
    value = jnp.sum(parts_ref[...], axis=0)
    for piece in range(16):
        out_ref[piece, :8] = value
        out_ref[piece, 8:] = kept_ref[...]


def unstack_spread(parts_ref, out_ref, kept_ref):
    spread(out_ref, jnp.sum(parts_ref[:, :8, :], axis=0))
    first = lax.axis_index("a") * 8
    on = jnp.where(lax.axis_index("x") == 0, 1.0, 0.0)
    for tile in range(2):
        blocks = [parts_ref[first + tile * 4 + i, 8:, :] for i in range(4)]
        for half in range(2):
            kept_ref[half * 2 + tile] = on * regroup([(block, half) for block in blocks])


def root_first(parts_ref, weights_ref, out_ref):
    operand = jnp.concatenate([parts_ref[i] for i in range(8)], axis=1)
    for step in range(4):
        weights = weights_ref[step * 4 : step * 4 + 4, :32, :].reshape(LANES, QUARTER)
        value = product(operand, weights, True)
        for row in range(8):
            out_ref[row * 4 + step] = value


def spread_product(out_ref, operand, weights_at):
    for step in range(4):
        value = product(operand, weights_at(step).reshape(LANES, QUARTER), True)
        for piece in range(out_ref.shape[0]):
            out_ref[piece, :, step * LANES : (step + 1) * LANES] = value


def root_second(parts_ref, weights_ref, out_ref):
    rows = sum_over_x(parts_ref)
    tiles = [regroup([(rows[(i % 2) * 4 + t], i // 2) for t in range(4)]) for i in range(8)]
    operand = jnp.concatenate(tiles, axis=1)
    spread_product(out_ref, operand, lambda step: weights_ref[step * 4 : step * 4 + 4, 32:64, :])


def pick_middle(parts_ref, index_ref, kept_ref, weights_ref, out_ref, rows_ref):
    rows = sum_over_x(parts_ref)
    for i in range(8):
        rows_ref[i] = rows[i]
    tiles = [rows[i // 4][:, (i % 4) * LANES : (i % 4 + 1) * LANES] for i in range(32)]
    picked = []
    for i in range(4):
        at = row_of(index_ref, i)
        plane = at >> 8
        tile_at = ((at >> 5) & 7) * 4 + (plane >> 2)
        picked.append(select_lanes(tiles, tile_at, (plane & 3) * 32 + (at & 31)))
    operand = jnp.concatenate(picked, axis=1)
    values = []
    first = lax.axis_index("a") * 8
    for half in range(2):
        lanes = slice(half * 512, (half + 1) * 512)
        weights = weights_ref[pl.ds(first, 8), 64:96, lanes].reshape(256, 512)
        coupled = product(operand, weights, True)
        for tile in range(2):
            values.append(kept_ref[half * 2 + tile] - coupled[:, tile * LANES : (tile + 1) * LANES])
    for to in range(4):
        low, high = values[to // 2], values[2 + to // 2]
        start = (to % 2) * 2
        value = regroup([(low, start), (low, start + 1), (high, start), (high, start + 1)])
        for row in range(8):
            out_ref[row * 4 + to] = value


def middle_second(parts_ref, weights_ref, out_ref):
    rows = sum_over_x(parts_ref)
    tiles = []
    for i in range(8):
        pair = [rows[(i % 4) * 2], rows[(i % 4) * 2 + 1]]
        tiles.append(regroup([(pair[g // 2], (g % 2) * 2 + i // 4) for g in range(4)]))
    operand = jnp.concatenate(tiles, axis=1)
    spread_product(out_ref, operand, lambda step: weights_ref[step * 2 : step * 2 + 2])


def pick_lower(parts_ref, index_ref, weights_ref, out_ref, rows_ref):
    rows = sum_over_x(parts_ref)
    for i in range(8):
        rows_ref[i] = rows[i]
    tiles = [rows[i // 4][:, (i % 4) * LANES : (i % 4 + 1) * LANES] for i in range(32)]
    picked = []
    for i in range(4):
        at = row_of(index_ref, i)
        tile_at = ((at >> 6) & 7) * 4 + (at >> 10)
        picked.append(select_lanes(tiles, tile_at, ((at >> 9) & 1) * 64 + (at & 63)))
    spread(out_ref, product(jnp.concatenate(picked, axis=1), weights_ref[...]))


def sources(positions):
    numbers = jnp.arange(512, dtype=jnp.int32)[:, None]
    hit = positions[:, None] == jnp.arange(S, dtype=jnp.int32)[None, :]
    return jnp.max(jnp.where(hit, numbers, -1), axis=0).reshape(32, LANES)


def placed(right_block, at):
    width = right_block.shape[1]
    times = LANES // width
    lanes = jnp.arange(LANES, dtype=jnp.int32)[None, :] // width
    here = (lanes == at % times) & (lax.axis_index("x") == 0)
    return jnp.where(here, jnp.tile(right_block, (1, times)), 0.0)


def local(
    right_root,
    right_middle,
    right_lower,
    inverse_root,
    inverse_middle,
    inverse_lower,
    upward_middle,
    upward_lower,
    downward_middle,
    downward_lower,
    index_middle,
    index_lower,
):
    at = lax.axis_index
    n = ("a", "b", "d", "y", "k")
    positions_middle = lax.dynamic_index_in_dim(index_middle, at("a"), 0, keepdims=False)
    positions_lower = lax.dynamic_index_in_dim(index_lower, at(("a", "b")), 0, keepdims=False)
    right_middle_tile = placed(right_middle, at(("b", "d", "y", "k")))
    right_root_tile = placed(right_root, at(n))
    source_lower = sources(positions_lower)
    source_middle = sources(positions_middle)

    parts, planes = call(
        start,
        [(32, 8, 128), (96, QUARTER)],
        right_lower,
        inverse_root.transpose(0, 2, 1),
        downward_middle.T,
    )
    planes = lax.all_gather(planes, ("a", "b", "d"), axis=0)

    parts = exchange(parts, "dyk")
    parts, middle_planes = call(
        lower_product_copy,
        [(4, 8, 128), (64, QUARTER)],
        parts,
        inverse_lower[0],
        inverse_middle.transpose(0, 2, 1),
        after=(source_lower, right_middle_tile),
    )
    middle_planes = lax.all_gather(middle_planes, ("b", "d"), axis=0)
    parts = exchange(parts, "x")
    parts, z_lower = call(
        functools.partial(extend, 128, 2),
        [(32, 8, 128), (8, 128)],
        parts,
        upward_lower,
        source_lower,
        right_middle_tile,
    )
    parts = exchange(parts, "ykx")
    parts = exchange(call(sum_spread, [(8, 8, 128)], parts), "bd")
    parts = exchange(call(sum_spread, [(8, 8, 128)], parts), "yk")
    parts = exchange(call(middle_product, [(4, 8, 128)], parts, inverse_middle[0].T), "x")
    parts, z_middle = call(
        functools.partial(extend, 64, 4),
        [(32, 8, 128), (8, 128)],
        parts,
        upward_middle,
        source_middle,
        right_root_tile,
    )
    parts = exchange(parts, "ykx")
    parts = exchange(call(stack_spread, [(16, 16, 128)], parts, z_middle), "abd")
    parts, z_middle = call(unstack_spread, [(8, 8, 128), (4, 8, 128)], parts, after=(planes[0, :8, :128],))
    parts = exchange(parts, "yk")
    parts = exchange(call(root_first, [(32, 8, 128)], parts, planes), "ykx")
    parts = exchange(call(root_second, [(32, 8, 512)], parts, planes), "ykx")
    parts, rows = call(
        pick_middle,
        [(32, 8, 128), (8, 8, 512)],
        parts,
        positions_middle.reshape(4, LANES),
        z_middle,
        planes,
    )
    row = lax.dynamic_index_in_dim(rows, at(("y", "k")), 0, keepdims=False)
    solution_root = lax.dynamic_slice_in_dim(row, at(("a", "b", "d")) * 32, 32, 1)
    parts = exchange(parts, "ykx")
    parts = exchange(call(middle_second, [(32, 8, 512)], parts, middle_planes), "ykx")
    parts, rows = call(
        pick_lower,
        [(4, 8, 128), (8, 8, 512)],
        parts,
        positions_lower.reshape(4, LANES),
        downward_lower,
    )
    row = lax.dynamic_index_in_dim(rows, at(("y", "k")), 0, keepdims=False)
    solution_middle = lax.dynamic_slice_in_dim(row, at(("b", "d")) * 64, 64, 1)
    parts = exchange(parts, "x")
    parts = exchange(call(subtract_spread, [(32, 8, 128)], parts, z_lower), "dyk")
    parts = exchange(call(lower_product, [(4, 8, 128)], parts, inverse_lower[1]), "x")
    solution_lower = call(sum_only, [(8, 128)], parts)
    return (solution_root, solution_middle, solution_lower)


def solution(mesh):
    split = Mesh(mesh.devices.reshape(tuple(SIZES.values())), tuple(SIZES))
    n = ("a", "b", "d", "y", "k")
    in_specs = (
        P(None, n),
        P(None, n),
        P(None, n),
        P(None, "x", n),
        P(None, "x", n),
        P(None, "x", n),
        P(n, "x"),
        P(n, "x"),
        P("x", n),
        P("x", n),
        P(None, "x"),
        P(None, "x"),
    )
    out_specs = (P(None, n), P(None, n), P(None, n))
    return jax.shard_map(local, mesh=split, in_specs=in_specs, out_specs=out_specs, check_vma=False)
```

time: 295 us -> 238 us (0.81)
  blocking collectives: 168 us -> 71.6 us
  starting transfers between devices: 37.3 us -> 57.5 us
  waiting for transfers between devices: 48.1 us -> 62.3 us
  other arithmetic: 17.8 us -> 3.75 us
  between operations: 1.05 us -> 14.3 us
  Pallas kernels: 0 us -> 12.2 us
  matrix products: 4.97 us -> 0 us
    all_to_all x14 -> x6, blocking collectives: 168 us -> 71.6 us  [exchange(): return lax.all_to_all(pieces, tuple(axes), 0, 0, tiled=False)]
    all_to_all x6 -> x10, starting transfers between devices: 37.3 us -> 57.4 us  [exchange(): return lax.all_to_all(pieces, tuple(axes), 0, 0, tiled=False)]
    all_to_all x6 -> x10, waiting for transfers between devices: 48.1 us -> 62.2 us  [exchange(): return lax.all_to_all(pieces, tuple(axes), 0, 0, tiled=False)]
    pallas_call x0 -> x17, Pallas kernels: none -> 12.2 us  [call(): pl.pallas_call(lambda *refs: body(*refs[extra:]), out_shape=shapes[0] if...]
    scatter-add x2 -> x0, other arithmetic: 8.12 us -> none  [extend(): update = update.at[:, positions].add(-product)]
    all_to_all x9 -> x0, other arithmetic: 6.38 us -> none  [exchange(): return lax.all_to_all(pieces, tuple(axes), 0, 0, tiled=False)]
    dot_general x10 -> x0, matrix products: 4.97 us -> none  [matmul_hi(): jnp.dot(left_side, right_side, precision=lax.Precision.HIGHEST, preferred...]
    reduce_max x0 -> x2, other arithmetic: none -> 3.72 us  [sources(): return jnp.max(jnp.where(hit, numbers, -1), axis=0).reshape(32, LANES)]
  transfers between devices with their start and end apart: 6 -> 12, of which waited for: 6 -> 10; matrix products, arithmetic and copies ran while one was open for 1% -> 4% of each run, Pallas kernels for 0% -> 3%
where the time goes in v2:
time: 238 us; the launch traced here: 236 us
  blocking collectives  71.6 us (30%)
  waiting for transfers between devices  62.3 us (26%)
  starting transfers between devices  57.5 us (24%)
  local copies, waits for them, and re-layouts  14.8 us (6%)
  between operations  14.3 us (6%)
  Pallas kernels  12.2 us (5%)
  other arithmetic  3.75 us (2%)
    all_to_all x6, blocking collectives, exchange(): return lax.all_to_all(pieces, tuple(axes), 0, 0, tiled=False)  71.6 us
    all_to_all x10, waiting for transfers between devices, exchange(): return lax.all_to_all(pieces, tuple(axes), 0, 0, tiled=False)  62.2 us
    all_to_all x10, starting transfers between devices, exchange(): return lax.all_to_all(pieces, tuple(axes), 0, 0, tiled=False)  57.4 us
    pallas_call x17, Pallas kernels, call(): pl.pallas_call(lambda *refs: body(*refs[extra:]), out_shape=shapes[0] if...  12.2 us
    unnamed x22, local copies, waits for them, and re-layouts  8.97 us
  transfers between devices with their start and end apart: 12, of which 10 were waited for; matrix products, arithmetic and copies ran while one was open for 4% of the time, Pallas kernels for 3%

profile of v2, /device:TPU:1, one launch (start us, length us, event | category | flops | bytes accessed | tf_op | source)
XLA Modules:
  0.0 236.4 jit_solution(9823001967642236500)
XLA Ops:
  10.7 10.4 %all-to-all-start = ((f32[32,8,128]{2,1,0:T(8,128)}), f32[32,8,128]{2,1,0:T(8,128)S(1)}, u32[]{:S(2)}, u32[]{:S(2)}) async-start(f32[32,8,128]{2,1,0:T(8,128)} %get-tuple-element.18), calls=%async_computation | async-start | bytes 262144 | tf_op jit(solution)/shard_map/all_to_all | solution.py:26
  25.1 4.6 %all-to-all-done.refs_2_ = f32[32,8,128]{2,1,0:T(8,128)S(1)} async-done(((f32[32,8,128]{2,1,0:T(8,128)}), f32[32,8,128]{2,1,0:T(8,128)S(1)}, u32[]{:S(2)}, u32[]{:S(2)}) %all-to-all-start) | async-done | bytes 131104 | tf_op jit(solution)/shard_map/all_to_all | solution.py:26
  31.6 3.7 %all-to-all-start.1 = ((f32[4,8,128]{2,1,0:T(8,128)}), f32[4,8,128]{2,1,0:T(8,128)S(1)}, u32[]{:S(2)}, u32[]{:S(2)}) async-start(f32[4,8,128]{2,1,0:T(8,128)} %get-tuple-element.19), calls=%async_computation.1 | async-start | bytes 32768 | tf_op jit(solution)/shard_map/all_to_all | solution.py:26
  36.1 3.6 %all-to-all-done.1.refs_0_ = f32[4,8,128]{2,1,0:T(8,128)S(1)} async-done(((f32[4,8,128]{2,1,0:T(8,128)}), f32[4,8,128]{2,1,0:T(8,128)S(1)}, u32[]{:S(2)}, u32[]{:S(2)}) %all-to-all-start.1) | async-done | bytes 16416 | tf_op jit(solution)/shard_map/all_to_all | solution.py:26
  41.8 5.3 %all-to-all-start.2 = ((f32[32,8,128]{2,1,0:T(8,128)}), f32[32,8,128]{2,1,0:T(8,128)S(1)}, u32[]{:S(2)}, u32[]{:S(2)}) async-start(f32[32,8,128]{2,1,0:T(8,128)} %get-tuple-element.20), calls=%async_computation.2 | async-start | bytes 262144 | tf_op jit(solution)/shard_map/all_to_all | solution.py:26
  48.9 5.8 %all-to-all-done.2.refs_0_ = f32[32,8,128]{2,1,0:T(8,128)S(1)} async-done(((f32[32,8,128]{2,1,0:T(8,128)}), f32[32,8,128]{2,1,0:T(8,128)S(1)}, u32[]{:S(2)}, u32[]{:S(2)}) %all-to-all-start.2) | async-done | bytes 131104 | tf_op jit(solution)/shard_map/all_to_all | solution.py:26
  55.4 8.9 %all-to-all-start.3 = ((f32[8,8,128]{2,1,0:T(8,128)}), f32[8,8,128]{2,1,0:T(8,128)S(1)}, u32[]{:S(2)}, u32[]{:S(2)}) async-start(f32[8,8,128]{2,1,0:T(8,128)} %shard_map.142), calls=%async_computation.3 | async-start | bytes 65536 | tf_op jit(solution)/shard_map/all_to_all | solution.py:26
  65.3 8.9 %all-to-all-done.3.refs_0_ = f32[8,8,128]{2,1,0:T(8,128)S(1)} async-done(((f32[8,8,128]{2,1,0:T(8,128)}), f32[8,8,128]{2,1,0:T(8,128)S(1)}, u32[]{:S(2)}, u32[]{:S(2)}) %all-to-all-start.3) | async-done | bytes 32800 | tf_op jit(solution)/shard_map/all_to_all | solution.py:26
  74.7 5.1 %all-to-all-start.4 = ((f32[8,8,128]{2,1,0:T(8,128)}), f32[8,8,128]{2,1,0:T(8,128)S(1)}, u32[]{:S(2)}, u32[]{:S(2)}) async-start(f32[8,8,128]{2,1,0:T(8,128)} %shard_map.143), calls=%async_computation.4 | async-start | bytes 65536 | tf_op jit(solution)/shard_map/all_to_all | solution.py:26
  79.9 4.7 %all-to-all-done.4.refs_0_ = f32[8,8,128]{2,1,0:T(8,128)S(1)} async-done(((f32[8,8,128]{2,1,0:T(8,128)}), f32[8,8,128]{2,1,0:T(8,128)S(1)}, u32[]{:S(2)}, u32[]{:S(2)}) %all-to-all-start.4) | async-done | bytes 32800 | tf_op jit(solution)/shard_map/all_to_all | solution.py:26
  88.7 4.2 %all-to-all-done.5.refs_0_ = f32[4,8,128]{2,1,0:T(8,128)S(1)} async-done(((f32[4,8,128]{2,1,0:T(8,128)}), f32[4,8,128]{2,1,0:T(8,128)S(1)}, u32[]{:S(2)}, u32[]{:S(2)}) %all-to-all-start.5) | async-done | bytes 16416 | tf_op jit(solution)/shard_map/all_to_all | solution.py:26
  93.5 12.4 %all_to_all.80.refs_0_ = f32[32,8,128]{2,1,0:T(8,128)S(1)} all-to-all(f32[32,8,128]{2,1,0:T(8,128)S(1)} %get-tuple-element.21), channel_id=1, replica_groups=mesh['a'=2,'b'=2,'d'=4,'y'=4,'k'=2,'x'=4] {'y','k','x'}, dimensions={0} | all-to-all | bytes 262144 | tf_op jit(solution)/shard_map/all_to_all | solution.py:26
  106.5 7.2 %all-to-all-start.7 = ((f32[16,16,128]{2,1,0:T(8,128)}), f32[16,16,128]{2,1,0:T(8,128)S(1)}, u32[]{:S(2)}, u32[]{:S(2)}) async-start(f32[16,16,128]{2,1,0:T(8,128)} %shard_map.146), calls=%async_computation.7 | async-start | bytes 262144 | tf_op jit(solution)/shard_map/all_to_all | solution.py:26
  114.5 11.5 %all-to-all-done.7.refs_1_ = f32[16,16,128]{2,1,0:T(8,128)S(1)} async-done(((f32[16,16,128]{2,1,0:T(8,128)}), f32[16,16,128]{2,1,0:T(8,128)S(1)}, u32[]{:S(2)}, u32[]{:S(2)}) %all-to-all-start.7) | async-done | bytes 131104 | tf_op jit(solution)/shard_map/all_to_all | solution.py:26
  126.0 10.7 %all_to_all.81.refs_0_ = f32[8,8,128]{2,1,0:T(8,128)S(1)} all-to-all(f32[8,8,128]{2,1,0:T(8,128)S(1)} %get-tuple-element.23), channel_id=1, replica_groups=mesh['a'=2,'b'=2,'d'=4,'y'=4,'k'=2,'x'=4] {'y','k'}, dimensions={0} | all-to-all | bytes 65536 | tf_op jit(solution)/shard_map/all_to_all | solution.py:26
  140.2 11.4 %all_to_all.82.refs_0_ = f32[32,8,128]{2,1,0:T(8,128)S(1)} all-to-all(f32[32,8,128]{2,1,0:T(8,128)S(1)} %shard_map.148), channel_id=1, replica_groups=mesh['a'=2,'b'=2,'d'=4,'y'=4,'k'=2,'x'=4] {'y','k','x'}, dimensions={0} | all-to-all | bytes 262144 | tf_op jit(solution)/shard_map/all_to_all | solution.py:26
  152.4 15.3 %all_to_all.83.refs_0_ = f32[32,8,512]{2,1,0:T(8,128)S(1)} all-to-all(f32[32,8,512]{2,1,0:T(8,128)S(1)} %shard_map.149), channel_id=1, replica_groups=mesh['a'=2,'b'=2,'d'=4,'y'=4,'k'=2,'x'=4] {'y','k','x'}, dimensions={0} | all-to-all | bytes 1048576 | tf_op jit(solution)/shard_map/all_to_all | solution.py:26
  169.0 4.3 %all-to-all-start.11 = ((f32[32,8,128]{2,1,0:T(8,128)}), f32[32,8,128]{2,1,0:T(8,128)S(1)}, u32[]{:S(2)}, u32[]{:S(2)}) async-start(f32[32,8,128]{2,1,0:T(8,128)} %get-tuple-element.26), calls=%async_computation.11 | async-start | bytes 262144 | tf_op jit(solution)/shard_map/all_to_all | solution.py:26
  173.3 7.6 %all-to-all-done.11.refs_0_ = f32[32,8,128]{2,1,0:T(8,128)S(1)} async-done(((f32[32,8,128]{2,1,0:T(8,128)}), f32[32,8,128]{2,1,0:T(8,128)S(1)}, u32[]{:S(2)}, u32[]{:S(2)}) %all-to-all-start.11) | async-done | bytes 131104 | tf_op jit(solution)/shard_map/all_to_all | solution.py:26
  183.2 15.2 %all_to_all.84.refs_0_ = f32[32,8,512]{2,1,0:T(8,128)S(1)} all-to-all(f32[32,8,512]{2,1,0:T(8,128)S(1)} %shard_map.151), channel_id=1, replica_groups=mesh['a'=2,'b'=2,'d'=4,'y'=4,'k'=2,'x'=4] {'y','k','x'}, dimensions={0} | all-to-all | bytes 1048576 | tf_op jit(solution)/shard_map/all_to_all | solution.py:26
  198.9 6.6 %all_to_all.85.refs_0_ = f32[4,8,128]{2,1,0:T(8,128)S(1)} all-to-all(f32[4,8,128]{2,1,0:T(8,128)S(1)} %get-tuple-element.29), channel_id=1, replica_groups=mesh['a'=2,'b'=2,'d'=4,'y'=4,'k'=2,'x'=4] {'x'}, dimensions={0} | all-to-all | bytes 32768 | tf_op jit(solution)/shard_map/all_to_all | solution.py:26
  206.1 6.1 %all-to-all-start.14 = ((f32[32,8,128]{2,1,0:T(8,128)}), f32[32,8,128]{2,1,0:T(8,128)S(1)}, u32[]{:S(2)}, u32[]{:S(2)}) async-start(f32[32,8,128]{2,1,0:T(8,128)} %shard_map.153), calls=%async_computation.14 | async-start | bytes 262144 | tf_op jit(solution)/shard_map/all_to_all | solution.py:26
  212.9 7.9 %all-to-all-done.14.refs_0_ = f32[32,8,128]{2,1,0:T(8,128)S(1)} async-done(((f32[32,8,128]{2,1,0:T(8,128)}), f32[32,8,128]{2,1,0:T(8,128)S(1)}, u32[]{:S(2)}, u32[]{:S(2)}) %all-to-all-start.14) | async-done | bytes 131104 | tf_op jit(solution)/shard_map/all_to_all | solution.py:26
  225.4 3.5 %all-to-all-done.15.refs_0_ = f32[4,8,128]{2,1,0:T(8,128)S(1)} async-done(((f32[4,8,128]{2,1,0:T(8,128)}), f32[4,8,128]{2,1,0:T(8,128)S(1)}, u32[]{:S(2)}, u32[]{:S(2)}) %all-to-all-start.15) | async-done | bytes 16416 | tf_op jit(solution)/shard_map/all_to_all | solution.py:26
  (64 shorter events, 37.3 us)
Async XLA Ops:
  7.2 14.8 %copy-start = (s32[4,512]{1,0:T(4,128)S(1)}, s32[4,512]{1,0:T(4,128)}, u32[]{:S(2)}) copy-start(s32[4,512]{1,0:T(4,128)} %param.23) | copy-start | bytes 24580
  7.2 106.6 %all-gather.5.cloned.1.call-start = ((), (), s32[]{:S(2)}) async-start(), calls=%async_computation.16 | async-start | bytes 6684672 | tf_op jit(solution)/shard_map/all_gather | solution.py:283
  7.2 1.0 copy-start.5
  8.2 0.9 copy-start.7
  9.1 0.7 copy-start.9
  9.8 70.1 %copy-start.10 = (f32[8,32]{1,0:T(8,128)S(1)}, f32[8,32]{1,0:T(8,128)}, u32[]{:S(2)}) copy-start(f32[8,32]{1,0:T(8,128)} %param.12) | copy-start | bytes 3076
  9.8 83.2 %copy-start.8 = (f32[64,512]{1,0:T(8,128)S(1)}, f32[64,512]{1,0:T(8,128)}, u32[]{:S(2)}) copy-start(f32[64,512]{1,0:T(8,128)} %refs_1_.3) | copy-start | bytes 393220
  10.7 19.1 %all-to-all-start = ((f32[32,8,128]{2,1,0:T(8,128)}), f32[32,8,128]{2,1,0:T(8,128)S(1)}, u32[]{:S(2)}, u32[]{:S(2)}) async-start(f32[32,8,128]{2,1,0:T(8,128)} %get-tuple-element.18), calls=%async_computation | async-start | bytes 262144 | tf_op jit(solution)/shard_map/all_to_all | solution.py:26
  21.1 152.2 %all-gather.7.cloned.1.call-start = ((), (), s32[]{:S(2)}) async-start(), calls=%async_computation.17 | async-start | bytes 2359296 | tf_op jit(solution)/shard_map/all_gather | solution.py:294
  29.8 1.0 copy-start.3
  31.6 8.0 %all-to-all-start.1 = ((f32[4,8,128]{2,1,0:T(8,128)}), f32[4,8,128]{2,1,0:T(8,128)S(1)}, u32[]{:S(2)}, u32[]{:S(2)}) async-start(f32[4,8,128]{2,1,0:T(8,128)} %get-tuple-element.19), calls=%async_computation.1 | async-start | bytes 32768 | tf_op jit(solution)/shard_map/all_to_all | solution.py:26
  39.6 1.0 copy-start.6
  41.8 13.0 %all-to-all-start.2 = ((f32[32,8,128]{2,1,0:T(8,128)}), f32[32,8,128]{2,1,0:T(8,128)S(1)}, u32[]{:S(2)}, u32[]{:S(2)}) async-start(f32[32,8,128]{2,1,0:T(8,128)} %get-tuple-element.20), calls=%async_computation.2 | async-start | bytes 262144 | tf_op jit(solution)/shard_map/all_to_all | solution.py:26
  55.4 18.7 %all-to-all-start.3 = ((f32[8,8,128]{2,1,0:T(8,128)}), f32[8,8,128]{2,1,0:T(8,128)S(1)}, u32[]{:S(2)}, u32[]{:S(2)}) async-start(f32[8,8,128]{2,1,0:T(8,128)} %shard_map.142), calls=%async_computation.3 | async-start | bytes 65536 | tf_op jit(solution)/shard_map/all_to_all | solution.py:26
  74.7 9.9 %all-to-all-start.4 = ((f32[8,8,128]{2,1,0:T(8,128)}), f32[8,8,128]{2,1,0:T(8,128)S(1)}, u32[]{:S(2)}, u32[]{:S(2)}) async-start(f32[8,8,128]{2,1,0:T(8,128)} %shard_map.143), calls=%async_computation.4 | async-start | bytes 65536 | tf_op jit(solution)/shard_map/all_to_all | solution.py:26
  85.5 7.5 %all-to-all-start.5 = ((f32[4,8,128]{2,1,0:T(8,128)}), f32[4,8,128]{2,1,0:T(8,128)S(1)}, u32[]{:S(2)}, u32[]{:S(2)}) async-start(f32[4,8,128]{2,1,0:T(8,128)} %shard_map.144), calls=%async_computation.5 | async-start | bytes 32768 | tf_op jit(solution)/shard_map/all_to_all | solution.py:26
  106.5 19.4 %all-to-all-start.7 = ((f32[16,16,128]{2,1,0:T(8,128)}), f32[16,16,128]{2,1,0:T(8,128)S(1)}, u32[]{:S(2)}, u32[]{:S(2)}) async-start(f32[16,16,128]{2,1,0:T(8,128)} %shard_map.146), calls=%async_computation.7 | async-start | bytes 262144 | tf_op jit(solution)/shard_map/all_to_all | solution.py:26
  136.7 2.8 %copy-start.1 = (f32[1536,1024]{1,0:T(8,128)S(1)}, f32[1536,1024]{1,0:T(8,128)}, u32[]{:S(2)}) copy-start(f32[1536,1024]{1,0:T(8,128)} %all-gather.5.cloned.1.call-done) | copy-start | bytes 18874372
  152.4 46.0 %copy-start.4 = (f32[512,128]{1,0:T(8,128)S(1)}, f32[512,128]{1,0:T(8,128)}, u32[]{:S(2)}) copy-start(f32[512,128]{1,0:T(8,128)} %refs_2_.1) | copy-start | bytes 786436
  169.0 11.9 %all-to-all-start.11 = ((f32[32,8,128]{2,1,0:T(8,128)}), f32[32,8,128]{2,1,0:T(8,128)S(1)}, u32[]{:S(2)}, u32[]{:S(2)}) async-start(f32[32,8,128]{2,1,0:T(8,128)} %get-tuple-element.26), calls=%async_computation.11 | async-start | bytes 262144 | tf_op jit(solution)/shard_map/all_to_all | solution.py:26
  180.8 1.6 copy-start.2
  206.1 14.6 %all-to-all-start.14 = ((f32[32,8,128]{2,1,0:T(8,128)}), f32[32,8,128]{2,1,0:T(8,128)S(1)}, u32[]{:S(2)}, u32[]{:S(2)}) async-start(f32[32,8,128]{2,1,0:T(8,128)} %shard_map.153), calls=%async_computation.14 | async-start | bytes 262144 | tf_op jit(solution)/shard_map/all_to_all | solution.py:26
  221.5 7.4 %all-to-all-start.15 = ((f32[4,8,128]{2,1,0:T(8,128)}), f32[4,8,128]{2,1,0:T(8,128)S(1)}, u32[]{:S(2)}, u32[]{:S(2)}) async-start(f32[4,8,128]{2,1,0:T(8,128)} %shard_map.154), calls=%async_computation.15 | async-start | bytes 32768 | tf_op jit(solution)/shard_map/all_to_all | solution.py:26
Sparse Core Ops, SparseCore 0:
  10.8 90.2 all-gather.4
  103.2 67.4 all-gather.6

commit v3 on v2

--- a/solution.py
+++ b/solution.py
@@ -1,5 +1,3 @@
-import functools
-
 import jax
 import jax.numpy as jnp
 from jax import lax
@@ -103,6 +101,16 @@
     return total
 
 
+def carve(planes_ref, first_ref, second_ref, coupling_ref):
+    first_ref[...] = planes_ref[:, :32, :]
+    second_ref[...] = planes_ref[:, 32:64, :]
+    coupling_ref[...] = planes_ref[pl.ds(lax.axis_index("a") * 8, 8), 64:, :]
+
+
+def hold(weights_ref, out_ref):
+    out_ref[...] = weights_ref[...]
+
+
 def start(right_ref, root_ref, coupling_ref, out_ref, planes_ref):
     spread(out_ref, right_ref[...])
     planes_ref[:32] = root_ref[0]
@@ -117,32 +125,52 @@
     spread(out_ref, product(operand, weights_ref[...]))
 
 
-def lower_product_copy(parts_ref, weights_ref, middle_ref, out_ref, copy_ref):
-    lower_product(parts_ref, weights_ref, out_ref)
+def lower_product_first(parts_ref, weights_ref, middle_ref, upward_ref, source_ref, out_ref, copy_ref):
     copy_ref[...] = middle_ref[1]
-
-
-def middle_product(parts_ref, weights_ref, out_ref):
-    operand = jnp.concatenate([parts_ref[i] for i in range(8)], axis=1)
-    doubled = jnp.concatenate([weights_ref[...], weights_ref[...]], axis=0)
-    spread(out_ref, product(operand, doubled, True))
-
-
-def extend(width, per_tile, parts_ref, weights_ref, source_ref, right_ref, out_ref, kept_ref):
-    value = jnp.sum(parts_ref[...], axis=0)
-    kept_ref[...] = value
-    update = product(value[:, :width], weights_ref[...])
-    tiles = [update[:, i * LANES : (i + 1) * LANES] for i in range(4)]
+    x_at = lax.axis_index("x")
+    operand = jnp.concatenate([parts_ref[x_at * 8 + i] for i in range(8)], axis=1)
+    value = product(operand, weights_ref[...])
+    source = source_ref[...].astype(jnp.float32)
+    for to in range(4):
+        out_ref[to, :8] = value
+        for tile in range(4):
+            rows = slice(8 + 64 * tile, 8 + 64 * (tile + 1))
+            out_ref[to, rows] = upward_ref[:, tile * LANES : (tile + 1) * LANES]
+        out_ref[to, 264:] = source
+
+
+def extend(tiles, sources, block_at, per_tile, right_ref, out_ref):
     for tile in range(32):
-        source = row_of(source_ref, tile)
+        source = jnp.broadcast_to(sources[tile : tile + 1], (8, LANES))
         out_ref[(tile % 8) * 4 + tile // 8] = -select_lanes(tiles, source >> 7, source & 127)
-    if per_tile == 2:
-        block_at = lax.axis_index(("b", "d", "y", "k"))
-    else:
-        block_at = lax.axis_index(("a", "b", "d", "y", "k"))
     tile_at = block_at // per_tile
     piece_at = (tile_at % 8) * 4 + tile_at // 8
     out_ref[piece_at] = out_ref[piece_at] + right_ref[...]
+
+
+def lower_extend(parts_ref, weights_ref, source_ref, right_ref, out_ref, kept_ref):
+    value = jnp.sum(parts_ref[:, :8, :], axis=0)
+    kept_ref[...] = value
+    update = product(value, weights_ref[...])
+    tiles = [update[:, i * LANES : (i + 1) * LANES] for i in range(4)]
+    extend(tiles, source_ref[...], lax.axis_index(("b", "d", "y", "k")), 2, right_ref, out_ref)
+
+
+def middle_extend(parts_ref, weights_ref, moved_ref, right_ref, out_ref, kept_ref):
+    operand = jnp.concatenate([parts_ref[i] for i in range(8)], axis=1)
+    doubled = jnp.concatenate([weights_ref[...], weights_ref[...]], axis=0)
+    value = product(operand, doubled, True)
+    kept_ref[...] = value
+    tiles = []
+    sources = jnp.full((32, LANES), -1.0, jnp.float32)
+    for x in range(4):
+        upward = [moved_ref[x, 8 + 64 * tile : 8 + 64 * (tile + 1), :] for tile in range(4)]
+        update = product(value[:, :64], jnp.concatenate(upward, axis=1))
+        tiles += [update[:, i * LANES : (i + 1) * LANES] for i in range(4)]
+        number = moved_ref[x, 264:, :]
+        sources = jnp.maximum(sources, jnp.where(number >= 0, number + 512.0 * x, -1.0))
+    sources = sources.astype(jnp.int32)
+    extend(tiles, sources, lax.axis_index(("a", "b", "d", "y", "k")), 4, right_ref, out_ref)
 
 
 def stack_spread(parts_ref, kept_ref, out_ref):
@@ -155,17 +183,16 @@
 def unstack_spread(parts_ref, out_ref, kept_ref):
     spread(out_ref, jnp.sum(parts_ref[:, :8, :], axis=0))
     first = lax.axis_index("a") * 8
-    on = jnp.where(lax.axis_index("x") == 0, 1.0, 0.0)
     for tile in range(2):
         blocks = [parts_ref[first + tile * 4 + i, 8:, :] for i in range(4)]
         for half in range(2):
-            kept_ref[half * 2 + tile] = on * regroup([(block, half) for block in blocks])
+            kept_ref[half * 2 + tile] = regroup([(block, half) for block in blocks])
 
 
 def root_first(parts_ref, weights_ref, out_ref):
     operand = jnp.concatenate([parts_ref[i] for i in range(8)], axis=1)
     for step in range(4):
-        weights = weights_ref[step * 4 : step * 4 + 4, :32, :].reshape(LANES, QUARTER)
+        weights = weights_ref[step * 4 : step * 4 + 4].reshape(LANES, QUARTER)
         value = product(operand, weights, True)
         for row in range(8):
             out_ref[row * 4 + step] = value
@@ -182,7 +209,7 @@
     rows = sum_over_x(parts_ref)
     tiles = [regroup([(rows[(i % 2) * 4 + t], i // 2) for t in range(4)]) for i in range(8)]
     operand = jnp.concatenate(tiles, axis=1)
-    spread_product(out_ref, operand, lambda step: weights_ref[step * 4 : step * 4 + 4, 32:64, :])
+    spread_product(out_ref, operand, lambda step: weights_ref[step * 4 : step * 4 + 4])
 
 
 def pick_middle(parts_ref, index_ref, kept_ref, weights_ref, out_ref, rows_ref):
@@ -198,10 +225,8 @@
         picked.append(select_lanes(tiles, tile_at, (plane & 3) * 32 + (at & 31)))
     operand = jnp.concatenate(picked, axis=1)
     values = []
-    first = lax.axis_index("a") * 8
     for half in range(2):
-        lanes = slice(half * 512, (half + 1) * 512)
-        weights = weights_ref[pl.ds(first, 8), 64:96, lanes].reshape(256, 512)
+        weights = weights_ref[:, :, half * 512 : (half + 1) * 512].reshape(256, 512)
         coupled = product(operand, weights, True)
         for tile in range(2):
             values.append(kept_ref[half * 2 + tile] - coupled[:, tile * LANES : (tile + 1) * LANES])
@@ -283,53 +308,53 @@
     planes = lax.all_gather(planes, ("a", "b", "d"), axis=0)
 
     parts = exchange(parts, "dyk")
-    parts, middle_planes = call(
-        lower_product_copy,
-        [(4, 8, 128), (64, QUARTER)],
+    moved, middle_planes = call(
+        lower_product_first,
+        [(4, 296, 128), (64, QUARTER)],
         parts,
         inverse_lower[0],
         inverse_middle.transpose(0, 2, 1),
+        upward_middle,
+        source_middle,
         after=(source_lower, right_middle_tile),
     )
     middle_planes = lax.all_gather(middle_planes, ("b", "d"), axis=0)
-    parts = exchange(parts, "x")
+    moved = exchange(moved, "x")
     parts, z_lower = call(
-        functools.partial(extend, 128, 2),
-        [(32, 8, 128), (8, 128)],
-        parts,
-        upward_lower,
-        source_lower,
-        right_middle_tile,
+        lower_extend, [(32, 8, 128), (8, 128)], moved, upward_lower, source_lower, right_middle_tile
     )
     parts = exchange(parts, "ykx")
     parts = exchange(call(sum_spread, [(8, 8, 128)], parts), "bd")
     parts = exchange(call(sum_spread, [(8, 8, 128)], parts), "yk")
-    parts = exchange(call(middle_product, [(4, 8, 128)], parts, inverse_middle[0].T), "x")
     parts, z_middle = call(
-        functools.partial(extend, 64, 4),
+        middle_extend,
         [(32, 8, 128), (8, 128)],
         parts,
-        upward_middle,
-        source_middle,
+        inverse_middle[0].T,
+        moved,
         right_root_tile,
     )
     parts = exchange(parts, "ykx")
     parts = exchange(call(stack_spread, [(16, 16, 128)], parts, z_middle), "abd")
-    parts, z_middle = call(unstack_spread, [(8, 8, 128), (4, 8, 128)], parts, after=(planes[0, :8, :128],))
+    first_weights, second_weights, coupling = call(
+        carve, [(16, 32, QUARTER), (16, 32, QUARTER), (8, 32, QUARTER)], planes
+    )
+    parts, z_middle = call(unstack_spread, [(8, 8, 128), (4, 8, 128)], parts, after=(first_weights,))
     parts = exchange(parts, "yk")
-    parts = exchange(call(root_first, [(32, 8, 128)], parts, planes), "ykx")
-    parts = exchange(call(root_second, [(32, 8, 512)], parts, planes), "ykx")
+    parts = exchange(call(root_first, [(32, 8, 128)], parts, first_weights), "ykx")
+    parts = exchange(call(root_second, [(32, 8, 512)], parts, second_weights), "ykx")
     parts, rows = call(
         pick_middle,
         [(32, 8, 128), (8, 8, 512)],
         parts,
         positions_middle.reshape(4, LANES),
         z_middle,
-        planes,
+        coupling,
     )
     row = lax.dynamic_index_in_dim(rows, at(("y", "k")), 0, keepdims=False)
     solution_root = lax.dynamic_slice_in_dim(row, at(("a", "b", "d")) * 32, 32, 1)
     parts = exchange(parts, "ykx")
+    middle_planes = call(hold, [(8, 64, QUARTER)], middle_planes)
     parts = exchange(call(middle_second, [(32, 8, 512)], parts, middle_planes), "ykx")
     parts, rows = call(
         pick_lower,

time: 238 us -> 233 us (0.979)
  blocking collectives: 71.6 us -> 97.2 us
  waiting for transfers between devices: 62.3 us -> 40.3 us
  starting transfers between devices: 57.5 us -> 46.9 us
    all_to_all x6 -> x8, blocking collectives: 71.6 us -> 97.2 us  [exchange(): return lax.all_to_all(pieces, tuple(axes), 0, 0, tiled=False)]
    all_to_all x10 -> x7, waiting for transfers between devices: 62.2 us -> 40.3 us  [exchange(): return lax.all_to_all(pieces, tuple(axes), 0, 0, tiled=False)]
    all_to_all x10 -> x7, starting transfers between devices: 57.4 us -> 46.8 us  [exchange(): return lax.all_to_all(pieces, tuple(axes), 0, 0, tiled=False)]
    unnamed x22 -> x32, local copies, waits for them, and re-layouts: 8.97 us -> 12.9 us
    pallas_call x17 -> x18, Pallas kernels: 12.2 us -> 12 us  [call(): pl.pallas_call(lambda *refs: body(*refs[extra:]), out_shape=shapes[0] if...]
  transfers between devices with their start and end apart: 12 -> 9, of which waited for: 10 -> 7; matrix products, arithmetic and copies ran while one was open for 4% -> 3% of each run, Pallas kernels for 3% -> 3%
where the time goes in v3:
time: 233 us; the launch traced here: 232 us
  blocking collectives  97.2 us (42%)
  starting transfers between devices  46.9 us (20%)
  waiting for transfers between devices  40.3 us (17%)
  local copies, waits for them, and re-layouts  17.1 us (7%)
  between operations  14.3 us (6%)
  Pallas kernels  12 us (5%)
  other arithmetic  3.75 us (2%)
    all_to_all x8, blocking collectives, exchange(): return lax.all_to_all(pieces, tuple(axes), 0, 0, tiled=False)  97.2 us
    all_to_all x7, starting transfers between devices, exchange(): return lax.all_to_all(pieces, tuple(axes), 0, 0, tiled=False)  46.8 us
    all_to_all x7, waiting for transfers between devices, exchange(): return lax.all_to_all(pieces, tuple(axes), 0, 0, tiled=False)  40.3 us
    unnamed x32, local copies, waits for them, and re-layouts  12.9 us
    pallas_call x18, Pallas kernels, call(): pl.pallas_call(lambda *refs: body(*refs[extra:]), out_shape=shapes[0] if...  12 us
  transfers between devices with their start and end apart: 9, of which 7 were waited for; matrix products, arithmetic and copies ran while one was open for 3% of the time, Pallas kernels for 3%

profile of v3, /device:TPU:1, one launch (start us, length us, event | category | flops | bytes accessed | tf_op | source)
XLA Modules:
  0.0 231.5 jit_solution(4496266771225586735)
XLA Ops:
  10.8 10.4 %all-to-all-start = ((f32[32,8,128]{2,1,0:T(8,128)}), f32[32,8,128]{2,1,0:T(8,128)S(1)}, u32[]{:S(2)}, u32[]{:S(2)}) async-start(f32[32,8,128]{2,1,0:T(8,128)} %get-tuple-element.22), calls=%async_computation | async-start | bytes 262144 | tf_op jit(solution)/shard_map/all_to_all | solution.py:24
  24.0 1.9 select_reduce_fusion.1
  27.8 2.1 all-to-all-done.refs_2_
  32.7 13.3 %all_to_all.75.refs_0_.refs_2_ = f32[4,296,128]{2,1,0:T(8,128)S(1)} all-to-all(f32[4,296,128]{2,1,0:T(8,128)S(1)} %get-tuple-element.23), channel_id=1, replica_groups=mesh['a'=2,'b'=2,'d'=4,'y'=4,'k'=2,'x'=4] {'x'}, dimensions={0} | all-to-all | bytes 1212416 | tf_op jit(solution)/shard_map/all_to_all | solution.py:24
  46.5 12.2 %all_to_all.76.refs_0_ = f32[32,8,128]{2,1,0:T(8,128)S(1)} all-to-all(f32[32,8,128]{2,1,0:T(8,128)S(1)} %get-tuple-element.24), channel_id=1, replica_groups=mesh['a'=2,'b'=2,'d'=4,'y'=4,'k'=2,'x'=4] {'y','k','x'}, dimensions={0} | all-to-all | bytes 262144 | tf_op jit(solution)/shard_map/all_to_all | solution.py:24
  59.4 10.9 %all-to-all-start.3 = ((f32[8,8,128]{2,1,0:T(8,128)}), f32[8,8,128]{2,1,0:T(8,128)S(1)}, u32[]{:S(2)}, u32[]{:S(2)}) async-start(f32[8,8,128]{2,1,0:T(8,128)} %shard_map.143), calls=%async_computation.3 | async-start | bytes 65536 | tf_op jit(solution)/shard_map/all_to_all | solution.py:24
  70.5 9.6 %all-to-all-done.3.refs_0_ = f32[8,8,128]{2,1,0:T(8,128)S(1)} async-done(((f32[8,8,128]{2,1,0:T(8,128)}), f32[8,8,128]{2,1,0:T(8,128)S(1)}, u32[]{:S(2)}, u32[]{:S(2)}) %all-to-all-start.3) | async-done | bytes 32800 | tf_op jit(solution)/shard_map/all_to_all | solution.py:24
  80.6 5.2 %all-to-all-start.4 = ((f32[8,8,128]{2,1,0:T(8,128)}), f32[8,8,128]{2,1,0:T(8,128)S(1)}, u32[]{:S(2)}, u32[]{:S(2)}) async-start(f32[8,8,128]{2,1,0:T(8,128)} %shard_map.144), calls=%async_computation.4 | async-start | bytes 65536 | tf_op jit(solution)/shard_map/all_to_all | solution.py:24
  85.8 4.8 %all-to-all-done.4.refs_0_ = f32[8,8,128]{2,1,0:T(8,128)S(1)} async-done(((f32[8,8,128]{2,1,0:T(8,128)}), f32[8,8,128]{2,1,0:T(8,128)S(1)}, u32[]{:S(2)}, u32[]{:S(2)}) %all-to-all-start.4) | async-done | bytes 32800 | tf_op jit(solution)/shard_map/all_to_all | solution.py:24
  91.9 11.8 %all_to_all.77.refs_0_ = f32[32,8,128]{2,1,0:T(8,128)S(1)} all-to-all(f32[32,8,128]{2,1,0:T(8,128)S(1)} %get-tuple-element.25), channel_id=1, replica_groups=mesh['a'=2,'b'=2,'d'=4,'y'=4,'k'=2,'x'=4] {'y','k','x'}, dimensions={0} | all-to-all | bytes 262144 | tf_op jit(solution)/shard_map/all_to_all | solution.py:24
  104.3 7.4 %all-to-all-start.6 = ((f32[16,16,128]{2,1,0:T(8,128)}), f32[16,16,128]{2,1,0:T(8,128)S(1)}, u32[]{:S(2)}, u32[]{:S(2)}) async-start(f32[16,16,128]{2,1,0:T(8,128)} %shard_map.146), calls=%async_computation.6 | async-start | bytes 262144 | tf_op jit(solution)/shard_map/all_to_all | solution.py:24
  111.8 2.8 %copy-done.1 = f32[1536,1024]{1,0:T(8,128)S(1)} copy-done((f32[1536,1024]{1,0:T(8,128)S(1)}, f32[1536,1024]{1,0:T(8,128)}, u32[]{:S(2)}) %copy-start.1) | copy-done | bytes 6291480
  117.2 6.6 %all-to-all-done.6.refs_1_ = f32[16,16,128]{2,1,0:T(8,128)S(1)} async-done(((f32[16,16,128]{2,1,0:T(8,128)}), f32[16,16,128]{2,1,0:T(8,128)S(1)}, u32[]{:S(2)}, u32[]{:S(2)}) %all-to-all-start.6) | async-done | bytes 131104 | tf_op jit(solution)/shard_map/all_to_all | solution.py:24
  124.0 10.8 %all_to_all.78.refs_0_ = f32[8,8,128]{2,1,0:T(8,128)S(1)} all-to-all(f32[8,8,128]{2,1,0:T(8,128)S(1)} %get-tuple-element.27), channel_id=1, replica_groups=mesh['a'=2,'b'=2,'d'=4,'y'=4,'k'=2,'x'=4] {'y','k'}, dimensions={0} | all-to-all | bytes 65536 | tf_op jit(solution)/shard_map/all_to_all | solution.py:24
  135.4 11.4 %all_to_all.79.refs_0_ = f32[32,8,128]{2,1,0:T(8,128)S(1)} all-to-all(f32[32,8,128]{2,1,0:T(8,128)S(1)} %shard_map.148), channel_id=1, replica_groups=mesh['a'=2,'b'=2,'d'=4,'y'=4,'k'=2,'x'=4] {'y','k','x'}, dimensions={0} | all-to-all | bytes 262144 | tf_op jit(solution)/shard_map/all_to_all | solution.py:24
  149.2 15.3 %all_to_all.80.refs_0_ = f32[32,8,512]{2,1,0:T(8,128)S(1)} all-to-all(f32[32,8,512]{2,1,0:T(8,128)S(1)} %shard_map.149), channel_id=1, replica_groups=mesh['a'=2,'b'=2,'d'=4,'y'=4,'k'=2,'x'=4] {'y','k','x'}, dimensions={0} | all-to-all | bytes 1048576 | tf_op jit(solution)/shard_map/all_to_all | solution.py:24
  165.8 4.1 %all-to-all-start.10 = ((f32[32,8,128]{2,1,0:T(8,128)}), f32[32,8,128]{2,1,0:T(8,128)S(1)}, u32[]{:S(2)}, u32[]{:S(2)}) async-start(f32[32,8,128]{2,1,0:T(8,128)} %get-tuple-element.32), calls=%async_computation.10 | async-start | bytes 262144 | tf_op jit(solution)/shard_map/all_to_all | solution.py:24
  171.7 5.9 %all-to-all-done.10.refs_0_ = f32[32,8,128]{2,1,0:T(8,128)S(1)} async-done(((f32[32,8,128]{2,1,0:T(8,128)}), f32[32,8,128]{2,1,0:T(8,128)S(1)}, u32[]{:S(2)}, u32[]{:S(2)}) %all-to-all-start.10) | async-done | bytes 131104 | tf_op jit(solution)/shard_map/all_to_all | solution.py:24
  178.3 15.8 %all_to_all.81.refs_0_ = f32[32,8,512]{2,1,0:T(8,128)S(1)} all-to-all(f32[32,8,512]{2,1,0:T(8,128)S(1)} %shard_map.152), channel_id=1, replica_groups=mesh['a'=2,'b'=2,'d'=4,'y'=4,'k'=2,'x'=4] {'y','k','x'}, dimensions={0} | all-to-all | bytes 1048576 | tf_op jit(solution)/shard_map/all_to_all | solution.py:24
  194.5 6.6 %all_to_all.82.refs_0_ = f32[4,8,128]{2,1,0:T(8,128)S(1)} all-to-all(f32[4,8,128]{2,1,0:T(8,128)S(1)} %get-tuple-element.35), channel_id=1, replica_groups=mesh['a'=2,'b'=2,'d'=4,'y'=4,'k'=2,'x'=4] {'x'}, dimensions={0} | all-to-all | bytes 32768 | tf_op jit(solution)/shard_map/all_to_all | solution.py:24
  201.7 5.6 %all-to-all-start.13 = ((f32[32,8,128]{2,1,0:T(8,128)}), f32[32,8,128]{2,1,0:T(8,128)S(1)}, u32[]{:S(2)}, u32[]{:S(2)}) async-start(f32[32,8,128]{2,1,0:T(8,128)} %shard_map.154), calls=%async_computation.13 | async-start | bytes 262144 | tf_op jit(solution)/shard_map/all_to_all | solution.py:24
  208.0 7.9 %all-to-all-done.13.refs_0_ = f32[32,8,128]{2,1,0:T(8,128)S(1)} async-done(((f32[32,8,128]{2,1,0:T(8,128)}), f32[32,8,128]{2,1,0:T(8,128)S(1)}, u32[]{:S(2)}, u32[]{:S(2)}) %all-to-all-start.13) | async-done | bytes 131104 | tf_op jit(solution)/shard_map/all_to_all | solution.py:24
  216.7 3.2 %all-to-all-start.14 = ((f32[4,8,128]{2,1,0:T(8,128)}), f32[4,8,128]{2,1,0:T(8,128)S(1)}, u32[]{:S(2)}, u32[]{:S(2)}) async-start(f32[4,8,128]{2,1,0:T(8,128)} %shard_map.155), calls=%async_computation.14 | async-start | bytes 32768 | tf_op jit(solution)/shard_map/all_to_all | solution.py:24
  220.6 3.5 %all-to-all-done.14.refs_0_ = f32[4,8,128]{2,1,0:T(8,128)S(1)} async-done(((f32[4,8,128]{2,1,0:T(8,128)}), f32[4,8,128]{2,1,0:T(8,128)S(1)}, u32[]{:S(2)}, u32[]{:S(2)}) %all-to-all-start.14) | async-done | bytes 16416 | tf_op jit(solution)/shard_map/all_to_all | solution.py:24
  (70 shorter events, 28.3 us)
Async XLA Ops:
  7.2 14.9 %copy-start = (s32[4,512]{1,0:T(4,128)S(1)}, s32[4,512]{1,0:T(4,128)}, u32[]{:S(2)}) copy-start(s32[4,512]{1,0:T(4,128)} %param.23) | copy-start | bytes 24580
  7.2 63.1 %copy-start.6 = (f32[2,1024,64]{1,2,0:T(8,128)S(1)}, f32[2,1024,64]{1,2,0:T(8,128)}, u32[]{:S(2)}) copy-start(f32[2,1024,64]{1,2,0:T(8,128)} %param.16) | copy-start | bytes 1572868
  7.2 38.8 %copy-start.9 = (f32[128,512]{1,0:T(8,128)S(1)}, f32[128,512]{1,0:T(8,128)}, u32[]{:S(2)}) copy-start(f32[128,512]{1,0:T(8,128)} %refs_1_.1) | copy-start | bytes 786436
  7.2 104.5 %all-gather.5.cloned.1.call-start = ((), (), s32[]{:S(2)}) async-start(), calls=%async_computation.15 | async-start | bytes 6684672 | tf_op jit(solution)/shard_map/all_gather | solution.py:308
  7.2 1.0 copy-start.11
  8.3 0.9 copy-start.12
  9.9 60.5 %copy-start.15 = (f32[8,32]{1,0:T(8,128)S(1)}, f32[8,32]{1,0:T(8,128)}, u32[]{:S(2)}) copy-start(f32[8,32]{1,0:T(8,128)} %param.12) | copy-start | bytes 3076
  10.8 19.1 %all-to-all-start = ((f32[32,8,128]{2,1,0:T(8,128)}), f32[32,8,128]{2,1,0:T(8,128)S(1)}, u32[]{:S(2)}, u32[]{:S(2)}) async-start(f32[32,8,128]{2,1,0:T(8,128)} %get-tuple-element.22), calls=%async_computation | async-start | bytes 262144 | tf_op jit(solution)/shard_map/all_to_all | solution.py:24
  21.2 148.7 %all-gather.7.cloned.1.call-start = ((), (), s32[]{:S(2)}) async-start(), calls=%async_computation.16 | async-start | bytes 2359296 | tf_op jit(solution)/shard_map/all_gather | solution.py:321
  29.9 1.0 copy-start.5
  30.9 0.9 copy-start.13
  59.4 20.6 %all-to-all-start.3 = ((f32[8,8,128]{2,1,0:T(8,128)}), f32[8,8,128]{2,1,0:T(8,128)S(1)}, u32[]{:S(2)}, u32[]{:S(2)}) async-start(f32[8,8,128]{2,1,0:T(8,128)} %shard_map.143), calls=%async_computation.3 | async-start | bytes 65536 | tf_op jit(solution)/shard_map/all_to_all | solution.py:24
  80.6 10.0 %all-to-all-start.4 = ((f32[8,8,128]{2,1,0:T(8,128)}), f32[8,8,128]{2,1,0:T(8,128)S(1)}, u32[]{:S(2)}, u32[]{:S(2)}) async-start(f32[8,8,128]{2,1,0:T(8,128)} %shard_map.144), calls=%async_computation.4 | async-start | bytes 65536 | tf_op jit(solution)/shard_map/all_to_all | solution.py:24
  104.3 19.5 %all-to-all-start.6 = ((f32[16,16,128]{2,1,0:T(8,128)}), f32[16,16,128]{2,1,0:T(8,128)S(1)}, u32[]{:S(2)}, u32[]{:S(2)}) async-start(f32[16,16,128]{2,1,0:T(8,128)} %shard_map.146), calls=%async_computation.6 | async-start | bytes 262144 | tf_op jit(solution)/shard_map/all_to_all | solution.py:24
  111.7 2.8 %copy-start.1 = (f32[1536,1024]{1,0:T(8,128)S(1)}, f32[1536,1024]{1,0:T(8,128)}, u32[]{:S(2)}) copy-start(f32[1536,1024]{1,0:T(8,128)} %all-gather.5.cloned.1.call-done) | copy-start | bytes 18874372
  114.9 1.4 copy-start.3
  116.2 1.0 copy-start.7
  123.9 40.7 %copy-start.8 = (f32[8,32,1024]{2,1,0:T(8,128)S(1)}, f32[8,32,1024]{2,1,0:T(8,128)}, u32[]{:S(2)}) copy-start(f32[8,32,1024]{2,1,0:T(8,128)} %copy-done.7) | copy-start | bytes 3145732
  146.9 1.6 copy-start.4
  148.5 45.5 %copy-start.10 = (f32[512,128]{1,0:T(8,128)S(1)}, f32[512,128]{1,0:T(8,128)}, u32[]{:S(2)}) copy-start(f32[512,128]{1,0:T(8,128)} %refs_2_.1) | copy-start | bytes 786436
  165.8 11.7 %all-to-all-start.10 = ((f32[32,8,128]{2,1,0:T(8,128)}), f32[32,8,128]{2,1,0:T(8,128)S(1)}, u32[]{:S(2)}, u32[]{:S(2)}) async-start(f32[32,8,128]{2,1,0:T(8,128)} %get-tuple-element.32), calls=%async_computation.10 | async-start | bytes 262144 | tf_op jit(solution)/shard_map/all_to_all | solution.py:24
  169.9 1.6 copy-start.2
  201.7 14.2 %all-to-all-start.13 = ((f32[32,8,128]{2,1,0:T(8,128)}), f32[32,8,128]{2,1,0:T(8,128)S(1)}, u32[]{:S(2)}, u32[]{:S(2)}) async-start(f32[32,8,128]{2,1,0:T(8,128)} %shard_map.154), calls=%async_computation.13 | async-start | bytes 262144 | tf_op jit(solution)/shard_map/all_to_all | solution.py:24
  216.7 7.4 %all-to-all-start.14 = ((f32[4,8,128]{2,1,0:T(8,128)}), f32[4,8,128]{2,1,0:T(8,128)S(1)}, u32[]{:S(2)}, u32[]{:S(2)}) async-start(f32[4,8,128]{2,1,0:T(8,128)} %shard_map.155), calls=%async_computation.14 | async-start | bytes 32768 | tf_op jit(solution)/shard_map/all_to_all | solution.py:24
  (1 other events, 0.7 us)
Sparse Core Ops, SparseCore 0:
  10.9 90.1 all-gather.4
  103.2 65.5 all-gather.6

commit v4 on v3

--- a/solution.py
+++ b/solution.py
@@ -111,14 +111,38 @@
     out_ref[...] = weights_ref[...]
 
 
-def start(right_ref, root_ref, coupling_ref, out_ref, planes_ref):
-    spread(out_ref, right_ref[...])
+def stack_planes(root_ref, coupling_ref, planes_ref):
     planes_ref[:32] = root_ref[0]
     planes_ref[32:64] = root_ref[1]
     planes_ref[64:, :512] = coupling_ref[:32]
     planes_ref[64:, 512:] = coupling_ref[32:]
 
 
+def spread_right(right_ref, out_ref):
+    spread(out_ref, right_ref[...])
+
+
+def map_sources(lower_ref, middle_ref, lower_out_ref, middle_out_ref):
+    for index_ref, out_ref in ((lower_ref, lower_out_ref), (middle_ref, middle_out_ref)):
+        index = jnp.concatenate([index_ref[i : i + 1, :] for i in range(4)], axis=1)
+        number = lax.broadcasted_iota(jnp.int32, (32, 512), 1) + 1
+        rows = jnp.broadcast_to(index >> 7, (32, 512)) == lax.broadcasted_iota(jnp.int32, (32, 512), 0)
+        lanes = jnp.broadcast_to(index & 127, (LANES, 512)) == lax.broadcasted_iota(jnp.int32, (LANES, 512), 0)
+        parts = [jnp.where(rows, part, 0).astype(jnp.float32) for part in (number >> 4, number & 15)]
+        found = lax.dot_general(
+            jnp.concatenate(parts, axis=0).astype(jnp.bfloat16),
+            jnp.where(lanes, 1.0, 0.0).astype(jnp.bfloat16),
+            (((1,), (1,)), ((), ())),
+            preferred_element_type=jnp.float32,
+        )
+        out_ref[...] = found[:32] * 16.0 + found[32:] - 1.0
+
+
+def hold_two(middle_ref, upward_ref, middle_out_ref, upward_out_ref):
+    middle_out_ref[...] = middle_ref[1]
+    upward_out_ref[...] = upward_ref[...]
+
+
 def lower_product(parts_ref, weights_ref, out_ref):
     x_at = lax.axis_index("x")
     operand = jnp.concatenate([parts_ref[x_at * 8 + i] for i in range(8)], axis=1)
@@ -126,11 +150,11 @@
 
 
 def lower_product_first(parts_ref, weights_ref, middle_ref, upward_ref, source_ref, out_ref, copy_ref):
-    copy_ref[...] = middle_ref[1]
+    copy_ref[...] = middle_ref[...]
     x_at = lax.axis_index("x")
     operand = jnp.concatenate([parts_ref[x_at * 8 + i] for i in range(8)], axis=1)
     value = product(operand, weights_ref[...])
-    source = source_ref[...].astype(jnp.float32)
+    source = source_ref[...]
     for to in range(4):
         out_ref[to, :8] = value
         for tile in range(4):
@@ -153,7 +177,7 @@
     kept_ref[...] = value
     update = product(value, weights_ref[...])
     tiles = [update[:, i * LANES : (i + 1) * LANES] for i in range(4)]
-    extend(tiles, source_ref[...], lax.axis_index(("b", "d", "y", "k")), 2, right_ref, out_ref)
+    extend(tiles, source_ref[...].astype(jnp.int32), lax.axis_index(("b", "d", "y", "k")), 2, right_ref, out_ref)
 
 
 def middle_extend(parts_ref, weights_ref, moved_ref, right_ref, out_ref, kept_ref):
@@ -261,12 +285,6 @@
     spread(out_ref, product(jnp.concatenate(picked, axis=1), weights_ref[...]))
 
 
-def sources(positions):
-    numbers = jnp.arange(512, dtype=jnp.int32)[:, None]
-    hit = positions[:, None] == jnp.arange(S, dtype=jnp.int32)[None, :]
-    return jnp.max(jnp.where(hit, numbers, -1), axis=0).reshape(32, LANES)
-
-
 def placed(right_block, at):
     width = right_block.shape[1]
     times = LANES // width
@@ -295,26 +313,32 @@
     positions_lower = lax.dynamic_index_in_dim(index_lower, at(("a", "b")), 0, keepdims=False)
     right_middle_tile = placed(right_middle, at(("b", "d", "y", "k")))
     right_root_tile = placed(right_root, at(n))
-    source_lower = sources(positions_lower)
-    source_middle = sources(positions_middle)
-
-    parts, planes = call(
-        start,
-        [(32, 8, 128), (96, QUARTER)],
-        right_lower,
-        inverse_root.transpose(0, 2, 1),
-        downward_middle.T,
-    )
+    source_lower, source_middle = call(
+        map_sources,
+        [(32, LANES), (32, LANES)],
+        positions_lower.reshape(4, LANES),
+        positions_middle.reshape(4, LANES),
+    )
+
+    planes = call(stack_planes, [(96, QUARTER)], inverse_root.transpose(0, 2, 1), downward_middle.T)
+    parts = call(spread_right, [(32, 8, 128)], right_lower, after=(planes,))
     planes = lax.all_gather(planes, ("a", "b", "d"), axis=0)
 
     parts = exchange(parts, "dyk")
+    middle_own, upward_own = call(
+        hold_two,
+        [(64, QUARTER), (64, 512)],
+        inverse_middle.transpose(0, 2, 1),
+        upward_middle,
+        after=(source_lower,),
+    )
     moved, middle_planes = call(
         lower_product_first,
         [(4, 296, 128), (64, QUARTER)],
         parts,
         inverse_lower[0],
-        inverse_middle.transpose(0, 2, 1),
-        upward_middle,
+        middle_own,
+        upward_own,
         source_middle,
         after=(source_lower, right_middle_tile),
     )

time: 233 us -> 232 us (level)
  blocking collectives: 97.2 us -> 101 us
  other arithmetic: 3.75 us -> 0.02 us
  waiting for transfers between devices: 40.3 us -> 44 us
  local copies, waits for them, and re-layouts: 17.1 us -> 13.6 us
  starting transfers between devices: 46.9 us -> 44.4 us
    all_to_all x8, blocking collectives: 97.2 us -> 101 us  [exchange(): return lax.all_to_all(pieces, tuple(axes), 0, 0, tiled=False)]
    reduce_max x2 -> x0, other arithmetic: 3.72 us -> none  [sources(): return jnp.max(jnp.where(hit, numbers, -1), axis=0).reshape(32, LANES)]
    unnamed x32 -> x30, local copies, waits for them, and re-layouts: 12.9 us -> 9.32 us
    all_to_all x7, starting transfers between devices: 46.8 us -> 44.3 us  [exchange(): return lax.all_to_all(pieces, tuple(axes), 0, 0, tiled=False)]
    pallas_call x18 -> x21, Pallas kernels: 12 us -> 12.8 us  [call(): pl.pallas_call(lambda *refs: body(*refs[extra:]), out_shape=shapes[0] if...]
  transfers between devices with their start and end apart: 9 -> 9, of which waited for: 7 -> 8; matrix products, arithmetic and copies ran while one was open for 3% -> 2% of each run, Pallas kernels for 3% -> 4%
where the time goes in v4:
time: 232 us; the launch traced here: 230 us
  blocking collectives  101 us (44%)
  starting transfers between devices  44.4 us (19%)
  waiting for transfers between devices  44 us (19%)
  between operations  14.3 us (6%)
  local copies, waits for them, and re-layouts  13.6 us (6%)
  Pallas kernels  12.8 us (6%)
    all_to_all x8, blocking collectives, exchange(): return lax.all_to_all(pieces, tuple(axes), 0, 0, tiled=False)  101 us
    all_to_all x7, starting transfers between devices, exchange(): return lax.all_to_all(pieces, tuple(axes), 0, 0, tiled=False)  44.3 us
    all_to_all x7, waiting for transfers between devices, exchange(): return lax.all_to_all(pieces, tuple(axes), 0, 0, tiled=False)  41.8 us
    pallas_call x21, Pallas kernels, call(): pl.pallas_call(lambda *refs: body(*refs[extra:]), out_shape=shapes[0] if...  12.8 us
    unnamed x30, local copies, waits for them, and re-layouts  9.32 us
  transfers between devices with their start and end apart: 9, of which 8 were waited for; matrix products, arithmetic and copies ran while one was open for 2% of the time, Pallas kernels for 4%

profile of v4, /device:TPU:1, one launch (start us, length us, event | category | flops | bytes accessed | tf_op | source)
XLA Modules:
  0.0 230.5 jit_solution(16169426919066100986)
XLA Ops:
  11.3 10.4 %all-to-all-start = ((f32[32,8,128]{2,1,0:T(8,128)}), f32[32,8,128]{2,1,0:T(8,128)S(1)}, u32[]{:S(2)}, u32[]{:S(2)}) async-start(f32[32,8,128]{2,1,0:T(8,128)} %shard_map.142), calls=%async_computation | async-start | bytes 262144 | tf_op jit(solution)/shard_map/all_to_all | solution.py:24
  24.9 5.4 %all-to-all-done.refs_2_ = f32[32,8,128]{2,1,0:T(8,128)S(1)} async-done(((f32[32,8,128]{2,1,0:T(8,128)}), f32[32,8,128]{2,1,0:T(8,128)S(1)}, u32[]{:S(2)}, u32[]{:S(2)}) %all-to-all-start) | async-done | bytes 131104 | tf_op jit(solution)/shard_map/all_to_all | solution.py:24
  31.2 13.3 %all_to_all.75.refs_0_.refs_2_ = f32[4,296,128]{2,1,0:T(8,128)S(1)} all-to-all(f32[4,296,128]{2,1,0:T(8,128)S(1)} %get-tuple-element.27), channel_id=1, replica_groups=mesh['a'=2,'b'=2,'d'=4,'y'=4,'k'=2,'x'=4] {'x'}, dimensions={0} | all-to-all | bytes 1212416 | tf_op jit(solution)/shard_map/all_to_all | solution.py:24
  45.0 12.2 %all_to_all.76.refs_0_ = f32[32,8,128]{2,1,0:T(8,128)S(1)} all-to-all(f32[32,8,128]{2,1,0:T(8,128)S(1)} %get-tuple-element.28), channel_id=1, replica_groups=mesh['a'=2,'b'=2,'d'=4,'y'=4,'k'=2,'x'=4] {'y','k','x'}, dimensions={0} | all-to-all | bytes 262144 | tf_op jit(solution)/shard_map/all_to_all | solution.py:24
  57.9 9.0 %all-to-all-start.3 = ((f32[8,8,128]{2,1,0:T(8,128)}), f32[8,8,128]{2,1,0:T(8,128)S(1)}, u32[]{:S(2)}, u32[]{:S(2)}) async-start(f32[8,8,128]{2,1,0:T(8,128)} %shard_map.146), calls=%async_computation.3 | async-start | bytes 65536 | tf_op jit(solution)/shard_map/all_to_all | solution.py:24
  67.0 9.7 %all-to-all-done.3.refs_0_ = f32[8,8,128]{2,1,0:T(8,128)S(1)} async-done(((f32[8,8,128]{2,1,0:T(8,128)}), f32[8,8,128]{2,1,0:T(8,128)S(1)}, u32[]{:S(2)}, u32[]{:S(2)}) %all-to-all-start.3) | async-done | bytes 32800 | tf_op jit(solution)/shard_map/all_to_all | solution.py:24
  77.3 5.1 %all-to-all-start.4 = ((f32[8,8,128]{2,1,0:T(8,128)}), f32[8,8,128]{2,1,0:T(8,128)S(1)}, u32[]{:S(2)}, u32[]{:S(2)}) async-start(f32[8,8,128]{2,1,0:T(8,128)} %shard_map.147), calls=%async_computation.4 | async-start | bytes 65536 | tf_op jit(solution)/shard_map/all_to_all | solution.py:24
  82.4 4.8 %all-to-all-done.4.refs_0_ = f32[8,8,128]{2,1,0:T(8,128)S(1)} async-done(((f32[8,8,128]{2,1,0:T(8,128)}), f32[8,8,128]{2,1,0:T(8,128)S(1)}, u32[]{:S(2)}, u32[]{:S(2)}) %all-to-all-start.4) | async-done | bytes 32800 | tf_op jit(solution)/shard_map/all_to_all | solution.py:24
  88.5 11.7 %all_to_all.77.refs_0_ = f32[32,8,128]{2,1,0:T(8,128)S(1)} all-to-all(f32[32,8,128]{2,1,0:T(8,128)S(1)} %get-tuple-element.29), channel_id=1, replica_groups=mesh['a'=2,'b'=2,'d'=4,'y'=4,'k'=2,'x'=4] {'y','k','x'}, dimensions={0} | all-to-all | bytes 262144 | tf_op jit(solution)/shard_map/all_to_all | solution.py:24
  100.9 7.4 %all-to-all-start.6 = ((f32[16,16,128]{2,1,0:T(8,128)}), f32[16,16,128]{2,1,0:T(8,128)S(1)}, u32[]{:S(2)}, u32[]{:S(2)}) async-start(f32[16,16,128]{2,1,0:T(8,128)} %shard_map.149), calls=%async_computation.6 | async-start | bytes 262144 | tf_op jit(solution)/shard_map/all_to_all | solution.py:24
  108.4 2.8 %copy-done.1 = f32[1536,1024]{1,0:T(8,128)S(1)} copy-done((f32[1536,1024]{1,0:T(8,128)S(1)}, f32[1536,1024]{1,0:T(8,128)}, u32[]{:S(2)}) %copy-start.1) | copy-done | bytes 6291480
  113.8 6.6 %all-to-all-done.6.refs_1_ = f32[16,16,128]{2,1,0:T(8,128)S(1)} async-done(((f32[16,16,128]{2,1,0:T(8,128)}), f32[16,16,128]{2,1,0:T(8,128)S(1)}, u32[]{:S(2)}, u32[]{:S(2)}) %all-to-all-start.6) | async-done | bytes 131104 | tf_op jit(solution)/shard_map/all_to_all | solution.py:24
  120.6 10.8 %all_to_all.78.refs_0_ = f32[8,8,128]{2,1,0:T(8,128)S(1)} all-to-all(f32[8,8,128]{2,1,0:T(8,128)S(1)} %get-tuple-element.31), channel_id=1, replica_groups=mesh['a'=2,'b'=2,'d'=4,'y'=4,'k'=2,'x'=4] {'y','k'}, dimensions={0} | all-to-all | bytes 65536 | tf_op jit(solution)/shard_map/all_to_all | solution.py:24
  132.0 11.8 %all_to_all.79.refs_0_ = f32[32,8,128]{2,1,0:T(8,128)S(1)} all-to-all(f32[32,8,128]{2,1,0:T(8,128)S(1)} %shard_map.151), channel_id=1, replica_groups=mesh['a'=2,'b'=2,'d'=4,'y'=4,'k'=2,'x'=4] {'y','k','x'}, dimensions={0} | all-to-all | bytes 262144 | tf_op jit(solution)/shard_map/all_to_all | solution.py:24
  144.6 15.2 %all_to_all.80.refs_0_ = f32[32,8,512]{2,1,0:T(8,128)S(1)} all-to-all(f32[32,8,512]{2,1,0:T(8,128)S(1)} %shard_map.152), channel_id=1, replica_groups=mesh['a'=2,'b'=2,'d'=4,'y'=4,'k'=2,'x'=4] {'y','k','x'}, dimensions={0} | all-to-all | bytes 1048576 | tf_op jit(solution)/shard_map/all_to_all | solution.py:24
  161.1 3.9 %all-to-all-start.10 = ((f32[32,8,128]{2,1,0:T(8,128)}), f32[32,8,128]{2,1,0:T(8,128)S(1)}, u32[]{:S(2)}, u32[]{:S(2)}) async-start(f32[32,8,128]{2,1,0:T(8,128)} %get-tuple-element.36), calls=%async_computation.10 | async-start | bytes 262144 | tf_op jit(solution)/shard_map/all_to_all | solution.py:24
  165.0 2.2 all-gather.7.cloned.1.call-done
  168.9 3.7 %all-to-all-done.10.refs_0_ = f32[32,8,128]{2,1,0:T(8,128)S(1)} async-done(((f32[32,8,128]{2,1,0:T(8,128)}), f32[32,8,128]{2,1,0:T(8,128)S(1)}, u32[]{:S(2)}, u32[]{:S(2)}) %all-to-all-start.10) | async-done | bytes 131104 | tf_op jit(solution)/shard_map/all_to_all | solution.py:24
  173.4 19.8 %all_to_all.81.refs_0_ = f32[32,8,512]{2,1,0:T(8,128)S(1)} all-to-all(f32[32,8,512]{2,1,0:T(8,128)S(1)} %shard_map.155), channel_id=1, replica_groups=mesh['a'=2,'b'=2,'d'=4,'y'=4,'k'=2,'x'=4] {'y','k','x'}, dimensions={0} | all-to-all | bytes 1048576 | tf_op jit(solution)/shard_map/all_to_all | solution.py:24
  193.6 6.6 %all_to_all.82.refs_0_ = f32[4,8,128]{2,1,0:T(8,128)S(1)} all-to-all(f32[4,8,128]{2,1,0:T(8,128)S(1)} %get-tuple-element.39), channel_id=1, replica_groups=mesh['a'=2,'b'=2,'d'=4,'y'=4,'k'=2,'x'=4] {'x'}, dimensions={0} | all-to-all | bytes 32768 | tf_op jit(solution)/shard_map/all_to_all | solution.py:24
  200.8 5.3 %all-to-all-start.13 = ((f32[32,8,128]{2,1,0:T(8,128)}), f32[32,8,128]{2,1,0:T(8,128)S(1)}, u32[]{:S(2)}, u32[]{:S(2)}) async-start(f32[32,8,128]{2,1,0:T(8,128)} %shard_map.157), calls=%async_computation.13 | async-start | bytes 262144 | tf_op jit(solution)/shard_map/all_to_all | solution.py:24
  206.8 8.0 %all-to-all-done.13.refs_0_ = f32[32,8,128]{2,1,0:T(8,128)S(1)} async-done(((f32[32,8,128]{2,1,0:T(8,128)}), f32[32,8,128]{2,1,0:T(8,128)S(1)}, u32[]{:S(2)}, u32[]{:S(2)}) %all-to-all-start.13) | async-done | bytes 131104 | tf_op jit(solution)/shard_map/all_to_all | solution.py:24
  215.6 3.2 %all-to-all-start.14 = ((f32[4,8,128]{2,1,0:T(8,128)}), f32[4,8,128]{2,1,0:T(8,128)S(1)}, u32[]{:S(2)}, u32[]{:S(2)}) async-start(f32[4,8,128]{2,1,0:T(8,128)} %shard_map.158), calls=%async_computation.14 | async-start | bytes 32768 | tf_op jit(solution)/shard_map/all_to_all | solution.py:24
  219.5 3.5 %all-to-all-done.14.refs_0_ = f32[4,8,128]{2,1,0:T(8,128)S(1)} async-done(((f32[4,8,128]{2,1,0:T(8,128)}), f32[4,8,128]{2,1,0:T(8,128)S(1)}, u32[]{:S(2)}, u32[]{:S(2)}) %all-to-all-start.14) | async-done | bytes 16416 | tf_op jit(solution)/shard_map/all_to_all | solution.py:24
  (69 shorter events, 23.7 us)
Async XLA Ops:
  7.2 14.6 %copy-start = (s32[4,512]{1,0:T(4,128)S(1)}, s32[4,512]{1,0:T(4,128)}, u32[]{:S(2)}) copy-start(s32[4,512]{1,0:T(4,128)} %param.23) | copy-start | bytes 24580
  7.2 16.3 %copy-start.5 = (f32[2,1024,64]{1,2,0:T(8,128)S(1)}, f32[2,1024,64]{1,2,0:T(8,128)}, u32[]{:S(2)}) copy-start(f32[2,1024,64]{1,2,0:T(8,128)} %param.16) | copy-start | bytes 1572868
  7.2 101.1 %all-gather.5.cloned.1.call-start = ((), (), s32[]{:S(2)}) async-start(), calls=%async_computation.15 | async-start | bytes 6684672 | tf_op jit(solution)/shard_map/all_gather | solution.py:325
  7.2 1.0 copy-start.8
  8.2 0.9 copy-start.11
  9.1 14.4 %copy-start.12 = (f32[64,512]{1,0:T(8,128)S(1)}, f32[64,512]{1,0:T(8,128)}, u32[]{:S(2)}) copy-start(f32[64,512]{1,0:T(8,128)} %refs_2_.2) | copy-start | bytes 393220
  10.0 0.7 copy-start.13
  11.3 19.0 %all-to-all-start = ((f32[32,8,128]{2,1,0:T(8,128)}), f32[32,8,128]{2,1,0:T(8,128)S(1)}, u32[]{:S(2)}, u32[]{:S(2)}) async-start(f32[32,8,128]{2,1,0:T(8,128)} %shard_map.142), calls=%async_computation | async-start | bytes 262144 | tf_op jit(solution)/shard_map/all_to_all | solution.py:24
  21.7 145.5 %all-gather.7.cloned.1.call-start = ((), (), s32[]{:S(2)}) async-start(), calls=%async_computation.16 | async-start | bytes 2359296 | tf_op jit(solution)/shard_map/all_gather | solution.py:345
  23.6 20.9 %copy-start.9 = (f32[128,512]{1,0:T(8,128)S(1)}, f32[128,512]{1,0:T(8,128)}, u32[]{:S(2)}) copy-start(f32[128,512]{1,0:T(8,128)} %refs_1_.3) | copy-start | bytes 786436
  30.3 36.6 %copy-start.14 = (f32[8,32]{1,0:T(8,128)S(1)}, f32[8,32]{1,0:T(8,128)}, u32[]{:S(2)}) copy-start(f32[8,32]{1,0:T(8,128)} %param.12) | copy-start | bytes 3076
  57.9 18.8 %all-to-all-start.3 = ((f32[8,8,128]{2,1,0:T(8,128)}), f32[8,8,128]{2,1,0:T(8,128)S(1)}, u32[]{:S(2)}, u32[]{:S(2)}) async-start(f32[8,8,128]{2,1,0:T(8,128)} %shard_map.146), calls=%async_computation.3 | async-start | bytes 65536 | tf_op jit(solution)/shard_map/all_to_all | solution.py:24
  77.3 9.9 %all-to-all-start.4 = ((f32[8,8,128]{2,1,0:T(8,128)}), f32[8,8,128]{2,1,0:T(8,128)S(1)}, u32[]{:S(2)}, u32[]{:S(2)}) async-start(f32[8,8,128]{2,1,0:T(8,128)} %shard_map.147), calls=%async_computation.4 | async-start | bytes 65536 | tf_op jit(solution)/shard_map/all_to_all | solution.py:24
  100.9 19.6 %all-to-all-start.6 = ((f32[16,16,128]{2,1,0:T(8,128)}), f32[16,16,128]{2,1,0:T(8,128)S(1)}, u32[]{:S(2)}, u32[]{:S(2)}) async-start(f32[16,16,128]{2,1,0:T(8,128)} %shard_map.149), calls=%async_computation.6 | async-start | bytes 262144 | tf_op jit(solution)/shard_map/all_to_all | solution.py:24
  108.3 2.8 %copy-start.1 = (f32[1536,1024]{1,0:T(8,128)S(1)}, f32[1536,1024]{1,0:T(8,128)}, u32[]{:S(2)}) copy-start(f32[1536,1024]{1,0:T(8,128)} %all-gather.5.cloned.1.call-done) | copy-start | bytes 18874372
  111.5 1.4 copy-start.3
  112.8 1.0 copy-start.6
  120.5 23.4 %copy-start.4 = (f32[16,32,1024]{2,1,0:T(8,128)S(1)}, f32[16,32,1024]{2,1,0:T(8,128)}, u32[]{:S(2)}) copy-start(f32[16,32,1024]{2,1,0:T(8,128)} %copy-done.3) | copy-start | bytes 6291460
  132.0 27.8 %copy-start.7 = (f32[8,32,1024]{2,1,0:T(8,128)S(1)}, f32[8,32,1024]{2,1,0:T(8,128)}, u32[]{:S(2)}) copy-start(f32[8,32,1024]{2,1,0:T(8,128)} %copy-done.6) | copy-start | bytes 3145732
  161.1 11.6 %all-to-all-start.10 = ((f32[32,8,128]{2,1,0:T(8,128)}), f32[32,8,128]{2,1,0:T(8,128)S(1)}, u32[]{:S(2)}, u32[]{:S(2)}) async-start(f32[32,8,128]{2,1,0:T(8,128)} %get-tuple-element.36), calls=%async_computation.10 | async-start | bytes 262144 | tf_op jit(solution)/shard_map/all_to_all | solution.py:24
  167.2 1.6 copy-start.2
  168.9 24.2 %copy-start.10 = (f32[512,128]{1,0:T(8,128)S(1)}, f32[512,128]{1,0:T(8,128)}, u32[]{:S(2)}) copy-start(f32[512,128]{1,0:T(8,128)} %refs_2_.3) | copy-start | bytes 786436
  200.8 14.0 %all-to-all-start.13 = ((f32[32,8,128]{2,1,0:T(8,128)}), f32[32,8,128]{2,1,0:T(8,128)S(1)}, u32[]{:S(2)}, u32[]{:S(2)}) async-start(f32[32,8,128]{2,1,0:T(8,128)} %shard_map.157), calls=%async_computation.13 | async-start | bytes 262144 | tf_op jit(solution)/shard_map/all_to_all | solution.py:24
  215.6 7.4 %all-to-all-start.14 = ((f32[4,8,128]{2,1,0:T(8,128)}), f32[4,8,128]{2,1,0:T(8,128)S(1)}, u32[]{:S(2)}, u32[]{:S(2)}) async-start(f32[4,8,128]{2,1,0:T(8,128)} %shard_map.158), calls=%async_computation.14 | async-start | bytes 32768 | tf_op jit(solution)/shard_map/all_to_all | solution.py:24
Sparse Core Ops, SparseCore 0:
  10.1 90.4 all-gather.4
  102.7 64.4 all-gather.6

commit v5 on v4

--- a/solution.py
+++ b/solution.py
@@ -74,10 +74,6 @@
 
 def sum_spread(parts_ref, out_ref):
     spread(out_ref, jnp.sum(parts_ref[...], axis=0))
-
-
-def sum_only(parts_ref, out_ref):
-    out_ref[...] = jnp.sum(parts_ref[...], axis=0)
 
 
 def subtract_spread(parts_ref, kept_ref, out_ref):
@@ -143,10 +139,10 @@
     upward_out_ref[...] = upward_ref[...]
 
 
-def lower_product(parts_ref, weights_ref, out_ref):
+def lower_last(parts_ref, weights_ref, out_ref):
     x_at = lax.axis_index("x")
     operand = jnp.concatenate([parts_ref[x_at * 8 + i] for i in range(8)], axis=1)
-    spread(out_ref, product(operand, weights_ref[...]))
+    out_ref[...] = product(operand, weights_ref[...])
 
 
 def lower_product_first(parts_ref, weights_ref, middle_ref, upward_ref, source_ref, out_ref, copy_ref):
@@ -391,8 +387,7 @@
     solution_middle = lax.dynamic_slice_in_dim(row, at(("b", "d")) * 64, 64, 1)
     parts = exchange(parts, "x")
     parts = exchange(call(subtract_spread, [(32, 8, 128)], parts, z_lower), "dyk")
-    parts = exchange(call(lower_product, [(4, 8, 128)], parts, inverse_lower[1]), "x")
-    solution_lower = call(sum_only, [(8, 128)], parts)
+    solution_lower = lax.psum(call(lower_last, [(8, 128)], parts, inverse_lower[1]), "x")
     return (solution_root, solution_middle, solution_lower)
 
 

time: 232 us -> 231 us (level)
  blocking collectives: 101 us -> 109 us
  waiting for transfers between devices: 44 us -> 39.8 us
  starting transfers between devices: 44.4 us -> 41.2 us
    psum x0 -> x1, blocking collectives: none -> 7.45 us  [local(): lax.psum(call(lower_last, [(8, 128)], parts, inverse_lower[1]), 'x')]
    all_to_all x7 -> x6, waiting for transfers between devices: 41.8 us -> 37.7 us  [exchange(): return lax.all_to_all(pieces, tuple(axes), 0, 0, tiled=False)]
    all_to_all x7 -> x6, starting transfers between devices: 44.3 us -> 41.1 us  [exchange(): return lax.all_to_all(pieces, tuple(axes), 0, 0, tiled=False)]
    pallas_call x21 -> x20, Pallas kernels: 12.8 us -> 11.7 us  [call(): pl.pallas_call(lambda *refs: body(*refs[extra:]), out_shape=shapes[0] if...]
  transfers between devices with their start and end apart: 9 -> 8, of which waited for: 8 -> 7; matrix products, arithmetic and copies ran while one was open for 2% -> 2% of each run, Pallas kernels for 4% -> 4%
where the time goes in v5:
time: 231 us; the launch traced here: 230 us
  blocking collectives  109 us (47%)
  starting transfers between devices  41.2 us (18%)
  waiting for transfers between devices  39.8 us (17%)
  between operations  14.3 us (6%)
  local copies, waits for them, and re-layouts  13.5 us (6%)
  Pallas kernels  11.7 us (5%)
    all_to_all x8, blocking collectives, exchange(): return lax.all_to_all(pieces, tuple(axes), 0, 0, tiled=False)  102 us
    all_to_all x6, starting transfers between devices, exchange(): return lax.all_to_all(pieces, tuple(axes), 0, 0, tiled=False)  41.1 us
    all_to_all x6, waiting for transfers between devices, exchange(): return lax.all_to_all(pieces, tuple(axes), 0, 0, tiled=False)  37.7 us
    pallas_call x20, Pallas kernels, call(): pl.pallas_call(lambda *refs: body(*refs[extra:]), out_shape=shapes[0] if...  11.7 us
    unnamed x30, local copies, waits for them, and re-layouts  9.31 us
    psum x1, blocking collectives, local(): lax.psum(call(lower_last, [(8, 128)], parts, inverse_lower[1]), 'x')  7.45 us
  transfers between devices with their start and end apart: 8, of which 7 were waited for; matrix products, arithmetic and copies ran while one was open for 2% of the time, Pallas kernels for 4%

profile of v5, /device:TPU:1, one launch (start us, length us, event | category | flops | bytes accessed | tf_op | source)
XLA Modules:
  0.0 229.6 jit_solution(9849477511167057237)
XLA Ops:
  11.3 10.4 %all-to-all-start = ((f32[32,8,128]{2,1,0:T(8,128)}), f32[32,8,128]{2,1,0:T(8,128)S(1)}, u32[]{:S(2)}, u32[]{:S(2)}) async-start(f32[32,8,128]{2,1,0:T(8,128)} %shard_map.142), calls=%async_computation | async-start | bytes 262144 | tf_op jit(solution)/shard_map/all_to_all | solution.py:24
  24.9 5.4 %all-to-all-done.refs_2_ = f32[32,8,128]{2,1,0:T(8,128)S(1)} async-done(((f32[32,8,128]{2,1,0:T(8,128)}), f32[32,8,128]{2,1,0:T(8,128)S(1)}, u32[]{:S(2)}, u32[]{:S(2)}) %all-to-all-start) | async-done | bytes 131104 | tf_op jit(solution)/shard_map/all_to_all | solution.py:24
  31.3 13.3 %all_to_all.70.refs_0_.refs_2_ = f32[4,296,128]{2,1,0:T(8,128)S(1)} all-to-all(f32[4,296,128]{2,1,0:T(8,128)S(1)} %get-tuple-element.27), channel_id=1, replica_groups=mesh['a'=2,'b'=2,'d'=4,'y'=4,'k'=2,'x'=4] {'x'}, dimensions={0} | all-to-all | bytes 1212416 | tf_op jit(solution)/shard_map/all_to_all | solution.py:24
  45.1 12.2 %all_to_all.71.refs_0_ = f32[32,8,128]{2,1,0:T(8,128)S(1)} all-to-all(f32[32,8,128]{2,1,0:T(8,128)S(1)} %get-tuple-element.28), channel_id=1, replica_groups=mesh['a'=2,'b'=2,'d'=4,'y'=4,'k'=2,'x'=4] {'y','k','x'}, dimensions={0} | all-to-all | bytes 262144 | tf_op jit(solution)/shard_map/all_to_all | solution.py:24
  58.0 9.0 %all-to-all-start.3 = ((f32[8,8,128]{2,1,0:T(8,128)}), f32[8,8,128]{2,1,0:T(8,128)S(1)}, u32[]{:S(2)}, u32[]{:S(2)}) async-start(f32[8,8,128]{2,1,0:T(8,128)} %shard_map.146), calls=%async_computation.3 | async-start | bytes 65536 | tf_op jit(solution)/shard_map/all_to_all | solution.py:24
  67.1 9.7 %all-to-all-done.3.refs_0_ = f32[8,8,128]{2,1,0:T(8,128)S(1)} async-done(((f32[8,8,128]{2,1,0:T(8,128)}), f32[8,8,128]{2,1,0:T(8,128)S(1)}, u32[]{:S(2)}, u32[]{:S(2)}) %all-to-all-start.3) | async-done | bytes 32800 | tf_op jit(solution)/shard_map/all_to_all | solution.py:24
  77.4 5.1 %all-to-all-start.4 = ((f32[8,8,128]{2,1,0:T(8,128)}), f32[8,8,128]{2,1,0:T(8,128)S(1)}, u32[]{:S(2)}, u32[]{:S(2)}) async-start(f32[8,8,128]{2,1,0:T(8,128)} %shard_map.147), calls=%async_computation.4 | async-start | bytes 65536 | tf_op jit(solution)/shard_map/all_to_all | solution.py:24
  82.5 4.8 %all-to-all-done.4.refs_0_ = f32[8,8,128]{2,1,0:T(8,128)S(1)} async-done(((f32[8,8,128]{2,1,0:T(8,128)}), f32[8,8,128]{2,1,0:T(8,128)S(1)}, u32[]{:S(2)}, u32[]{:S(2)}) %all-to-all-start.4) | async-done | bytes 32800 | tf_op jit(solution)/shard_map/all_to_all | solution.py:24
  88.6 11.7 %all_to_all.72.refs_0_ = f32[32,8,128]{2,1,0:T(8,128)S(1)} all-to-all(f32[32,8,128]{2,1,0:T(8,128)S(1)} %get-tuple-element.29), channel_id=1, replica_groups=mesh['a'=2,'b'=2,'d'=4,'y'=4,'k'=2,'x'=4] {'y','k','x'}, dimensions={0} | all-to-all | bytes 262144 | tf_op jit(solution)/shard_map/all_to_all | solution.py:24
  101.0 7.4 %all-to-all-start.6 = ((f32[16,16,128]{2,1,0:T(8,128)}), f32[16,16,128]{2,1,0:T(8,128)S(1)}, u32[]{:S(2)}, u32[]{:S(2)}) async-start(f32[16,16,128]{2,1,0:T(8,128)} %shard_map.149), calls=%async_computation.6 | async-start | bytes 262144 | tf_op jit(solution)/shard_map/all_to_all | solution.py:24
  108.4 2.8 %copy-done.1 = f32[1536,1024]{1,0:T(8,128)S(1)} copy-done((f32[1536,1024]{1,0:T(8,128)S(1)}, f32[1536,1024]{1,0:T(8,128)}, u32[]{:S(2)}) %copy-start.1) | copy-done | bytes 6291480
  113.9 6.7 %all-to-all-done.6.refs_1_ = f32[16,16,128]{2,1,0:T(8,128)S(1)} async-done(((f32[16,16,128]{2,1,0:T(8,128)}), f32[16,16,128]{2,1,0:T(8,128)S(1)}, u32[]{:S(2)}, u32[]{:S(2)}) %all-to-all-start.6) | async-done | bytes 131104 | tf_op jit(solution)/shard_map/all_to_all | solution.py:24
  120.6 10.8 %all_to_all.73.refs_0_ = f32[8,8,128]{2,1,0:T(8,128)S(1)} all-to-all(f32[8,8,128]{2,1,0:T(8,128)S(1)} %get-tuple-element.31), channel_id=1, replica_groups=mesh['a'=2,'b'=2,'d'=4,'y'=4,'k'=2,'x'=4] {'y','k'}, dimensions={0} | all-to-all | bytes 65536 | tf_op jit(solution)/shard_map/all_to_all | solution.py:24
  132.1 11.8 %all_to_all.74.refs_0_ = f32[32,8,128]{2,1,0:T(8,128)S(1)} all-to-all(f32[32,8,128]{2,1,0:T(8,128)S(1)} %shard_map.151), channel_id=1, replica_groups=mesh['a'=2,'b'=2,'d'=4,'y'=4,'k'=2,'x'=4] {'y','k','x'}, dimensions={0} | all-to-all | bytes 262144 | tf_op jit(solution)/shard_map/all_to_all | solution.py:24
  144.6 15.2 %all_to_all.75.refs_0_ = f32[32,8,512]{2,1,0:T(8,128)S(1)} all-to-all(f32[32,8,512]{2,1,0:T(8,128)S(1)} %shard_map.152), channel_id=1, replica_groups=mesh['a'=2,'b'=2,'d'=4,'y'=4,'k'=2,'x'=4] {'y','k','x'}, dimensions={0} | all-to-all | bytes 1048576 | tf_op jit(solution)/shard_map/all_to_all | solution.py:24
  161.1 3.9 %all-to-all-start.10 = ((f32[32,8,128]{2,1,0:T(8,128)}), f32[32,8,128]{2,1,0:T(8,128)S(1)}, u32[]{:S(2)}, u32[]{:S(2)}) async-start(f32[32,8,128]{2,1,0:T(8,128)} %get-tuple-element.36), calls=%async_computation.10 | async-start | bytes 262144 | tf_op jit(solution)/shard_map/all_to_all | solution.py:24
  165.1 2.0 all-gather.7.cloned.1.call-done
  167.1 1.6 copy-done.2
  168.8 3.8 %all-to-all-done.10.refs_0_ = f32[32,8,128]{2,1,0:T(8,128)S(1)} async-done(((f32[32,8,128]{2,1,0:T(8,128)}), f32[32,8,128]{2,1,0:T(8,128)S(1)}, u32[]{:S(2)}, u32[]{:S(2)}) %all-to-all-start.10) | async-done | bytes 131104 | tf_op jit(solution)/shard_map/all_to_all | solution.py:24
  173.4 20.0 %all_to_all.76.refs_0_ = f32[32,8,512]{2,1,0:T(8,128)S(1)} all-to-all(f32[32,8,512]{2,1,0:T(8,128)S(1)} %shard_map.155), channel_id=1, replica_groups=mesh['a'=2,'b'=2,'d'=4,'y'=4,'k'=2,'x'=4] {'y','k','x'}, dimensions={0} | all-to-all | bytes 1048576 | tf_op jit(solution)/shard_map/all_to_all | solution.py:24
  193.9 6.6 %all_to_all.77.refs_0_ = f32[4,8,128]{2,1,0:T(8,128)S(1)} all-to-all(f32[4,8,128]{2,1,0:T(8,128)S(1)} %get-tuple-element.39), channel_id=1, replica_groups=mesh['a'=2,'b'=2,'d'=4,'y'=4,'k'=2,'x'=4] {'x'}, dimensions={0} | all-to-all | bytes 32768 | tf_op jit(solution)/shard_map/all_to_all | solution.py:24
  201.1 5.3 %all-to-all-start.13 = ((f32[32,8,128]{2,1,0:T(8,128)}), f32[32,8,128]{2,1,0:T(8,128)S(1)}, u32[]{:S(2)}, u32[]{:S(2)}) async-start(f32[32,8,128]{2,1,0:T(8,128)} %shard_map.157), calls=%async_computation.13 | async-start | bytes 262144 | tf_op jit(solution)/shard_map/all_to_all | solution.py:24
  207.8 7.3 %all-to-all-done.13.refs_0_ = f32[32,8,128]{2,1,0:T(8,128)S(1)} async-done(((f32[32,8,128]{2,1,0:T(8,128)}), f32[32,8,128]{2,1,0:T(8,128)S(1)}, u32[]{:S(2)}, u32[]{:S(2)}) %all-to-all-start.13) | async-done | bytes 131104 | tf_op jit(solution)/shard_map/all_to_all | solution.py:24
  215.3 7.5 %psum.7 = f32[8,128]{1,0:T(8,128)} all-reduce(f32[8,128]{1,0:T(8,128)S(1)} %shard_map.158), channel_id=1, replica_groups=mesh['a'=2,'b'=2,'d'=4,'y'=4,'k'=2,'x'=4] {'x'}, use_global_device_ids=true, to_apply=%region_0.1 | all-reduce | flops 1024 | bytes 8192 | tf_op jit(solution)/shard_map/psum | solution.py:390
  (67 shorter events, 21.0 us)
Async XLA Ops:
  7.2 14.6 %copy-start = (s32[4,512]{1,0:T(4,128)S(1)}, s32[4,512]{1,0:T(4,128)}, u32[]{:S(2)}) copy-start(s32[4,512]{1,0:T(4,128)} %param.23) | copy-start | bytes 24580
  7.2 16.4 %copy-start.5 = (f32[2,1024,64]{1,2,0:T(8,128)S(1)}, f32[2,1024,64]{1,2,0:T(8,128)}, u32[]{:S(2)}) copy-start(f32[2,1024,64]{1,2,0:T(8,128)} %param.16) | copy-start | bytes 1572868
  7.2 101.2 %all-gather.5.cloned.1.call-start = ((), (), s32[]{:S(2)}) async-start(), calls=%async_computation.14 | async-start | bytes 6684672 | tf_op jit(solution)/shard_map/all_gather | solution.py:321
  7.2 1.0 copy-start.8
  8.2 0.9 copy-start.11
  9.1 14.4 %copy-start.12 = (f32[64,512]{1,0:T(8,128)S(1)}, f32[64,512]{1,0:T(8,128)}, u32[]{:S(2)}) copy-start(f32[64,512]{1,0:T(8,128)} %refs_2_.2) | copy-start | bytes 393220
  10.0 0.7 copy-start.13
  11.3 19.0 %all-to-all-start = ((f32[32,8,128]{2,1,0:T(8,128)}), f32[32,8,128]{2,1,0:T(8,128)S(1)}, u32[]{:S(2)}, u32[]{:S(2)}) async-start(f32[32,8,128]{2,1,0:T(8,128)} %shard_map.142), calls=%async_computation | async-start | bytes 262144 | tf_op jit(solution)/shard_map/all_to_all | solution.py:24
  21.7 145.4 %all-gather.7.cloned.1.call-start = ((), (), s32[]{:S(2)}) async-start(), calls=%async_computation.15 | async-start | bytes 2359296 | tf_op jit(solution)/shard_map/all_gather | solution.py:341
  23.6 20.9 %copy-start.9 = (f32[128,512]{1,0:T(8,128)S(1)}, f32[128,512]{1,0:T(8,128)}, u32[]{:S(2)}) copy-start(f32[128,512]{1,0:T(8,128)} %refs_1_.3) | copy-start | bytes 786436
  30.4 36.6 %copy-start.14 = (f32[8,32]{1,0:T(8,128)S(1)}, f32[8,32]{1,0:T(8,128)}, u32[]{:S(2)}) copy-start(f32[8,32]{1,0:T(8,128)} %param.12) | copy-start | bytes 3076
  58.0 18.8 %all-to-all-start.3 = ((f32[8,8,128]{2,1,0:T(8,128)}), f32[8,8,128]{2,1,0:T(8,128)S(1)}, u32[]{:S(2)}, u32[]{:S(2)}) async-start(f32[8,8,128]{2,1,0:T(8,128)} %shard_map.146), calls=%async_computation.3 | async-start | bytes 65536 | tf_op jit(solution)/shard_map/all_to_all | solution.py:24
  77.4 9.9 %all-to-all-start.4 = ((f32[8,8,128]{2,1,0:T(8,128)}), f32[8,8,128]{2,1,0:T(8,128)S(1)}, u32[]{:S(2)}, u32[]{:S(2)}) async-start(f32[8,8,128]{2,1,0:T(8,128)} %shard_map.147), calls=%async_computation.4 | async-start | bytes 65536 | tf_op jit(solution)/shard_map/all_to_all | solution.py:24
  101.0 19.6 %all-to-all-start.6 = ((f32[16,16,128]{2,1,0:T(8,128)}), f32[16,16,128]{2,1,0:T(8,128)S(1)}, u32[]{:S(2)}, u32[]{:S(2)}) async-start(f32[16,16,128]{2,1,0:T(8,128)} %shard_map.149), calls=%async_computation.6 | async-start | bytes 262144 | tf_op jit(solution)/shard_map/all_to_all | solution.py:24
  108.4 2.8 %copy-start.1 = (f32[1536,1024]{1,0:T(8,128)S(1)}, f32[1536,1024]{1,0:T(8,128)}, u32[]{:S(2)}) copy-start(f32[1536,1024]{1,0:T(8,128)} %all-gather.5.cloned.1.call-done) | copy-start | bytes 18874372
  111.6 1.4 copy-start.3
  112.9 1.0 copy-start.6
  120.5 23.3 %copy-start.4 = (f32[16,32,1024]{2,1,0:T(8,128)S(1)}, f32[16,32,1024]{2,1,0:T(8,128)}, u32[]{:S(2)}) copy-start(f32[16,32,1024]{2,1,0:T(8,128)} %copy-done.3) | copy-start | bytes 6291460
  132.1 27.7 %copy-start.7 = (f32[8,32,1024]{2,1,0:T(8,128)S(1)}, f32[8,32,1024]{2,1,0:T(8,128)}, u32[]{:S(2)}) copy-start(f32[8,32,1024]{2,1,0:T(8,128)} %copy-done.6) | copy-start | bytes 3145732
  161.1 11.6 %all-to-all-start.10 = ((f32[32,8,128]{2,1,0:T(8,128)}), f32[32,8,128]{2,1,0:T(8,128)S(1)}, u32[]{:S(2)}, u32[]{:S(2)}) async-start(f32[32,8,128]{2,1,0:T(8,128)} %get-tuple-element.36), calls=%async_computation.10 | async-start | bytes 262144 | tf_op jit(solution)/shard_map/all_to_all | solution.py:24
  167.1 1.6 copy-start.2
  168.8 24.6 %copy-start.10 = (f32[512,128]{1,0:T(8,128)S(1)}, f32[512,128]{1,0:T(8,128)}, u32[]{:S(2)}) copy-start(f32[512,128]{1,0:T(8,128)} %refs_2_.3) | copy-start | bytes 786436
  201.1 14.0 %all-to-all-start.13 = ((f32[32,8,128]{2,1,0:T(8,128)}), f32[32,8,128]{2,1,0:T(8,128)S(1)}, u32[]{:S(2)}, u32[]{:S(2)}) async-start(f32[32,8,128]{2,1,0:T(8,128)} %shard_map.157), calls=%async_computation.13 | async-start | bytes 262144 | tf_op jit(solution)/shard_map/all_to_all | solution.py:24
Sparse Core Ops, SparseCore 0:
  10.1 90.2 all-gather.4
  102.5 64.5 all-gather.6
